TPU v7x, 128 devices: a whole 4x4x4 slice. The times are simulated.
128 devices in a mesh: rep: 2 (over x_lo), ep: 64 (over y, z, x_hi, core).
Axes of the slice: x: 4 (x_hi: 2, x_lo: 2; x = x_hi * 2 + x_lo), y: 4, z: 4, core: 2. Of those that a mesh axis runs over, the one named last changes fastest.
Arguments:
- query_nope: bfloat16 [2048, 8192], P(('rep', 'ep')), may hold values from -6 to 6
- query_rope: bfloat16 [2048, 4096], P(('rep', 'ep')), may hold values from -150 to 150
- query_compressed: bfloat16 [2048, 1536], P(('rep', 'ep')), may hold values from -6 to 6
- kv_cache: bfloat16 [2048, 192, 576], P(('rep', 'ep')), may hold values from -8 to 8
- cache_lengths: int32 [2048], P(('rep', 'ep')), may hold values from 2 to 192
- key_base: bfloat16 [64, 128, 512], P('rep'), may hold values from -0.25 to 0.25
- query_down: bfloat16 [2, 1536, 64], P('rep'), may hold values from -0.15625 to 0.15625
- query_rise: bfloat16 [2, 64, 8192], P('rep'), may hold values from -0.75 to 0.75
- key_down: bfloat16 [2, 64, 512], P('rep'), may hold values from -0.25 to 0.25
- key_rise: bfloat16 [2, 64, 8192], P('rep'), may hold values from -0.75 to 0.75
- moe_input: bfloat16 [2048, 3584], P(('rep', 'ep')), may hold values from -6 to 6
- expert_ids: int32 [2048, 8], P(('rep', 'ep')), may hold values from 0 to 127, all different within a row; in each aligned block of 16 rows (0 to 15, 16 to 31, ...) at most 3 rows name the same one
- route_weights: float32 [2048, 8], P(('rep', 'ep')), may hold values from 0.1 to 1
- expert_gate_up: bfloat16 [128, 3584, 2048], P(('rep', 'ep')), may hold values from -0.09375 to 0.09375
Outputs:
- attended: bfloat16 [2048, 32768], P(('rep', 'ep'))
- expert_hidden: bfloat16 [2048, 8192], P(('rep', 'ep'))
Inputs may be any that keep to these rules, and one draw needn't show every extreme that they name: `expert_ids`: A row names 8 different experts; among the rows of one device no expert is named by more than 3 rows, a bound that some block reaches.
All inputs are finite; a program needn't handle non-finite values.
Results may differ from a plain program's by a relative error of at most 0.0077.
Values may be sent and summed in bfloat16 or wider, within the bound.
No kernel may reach another device: no remote copies, remote signals or barrier semaphores. Data moves between devices by JAX's collectives and lax.ppermute only.
A program may use at most 128 MiB of HBM per device.

v0:
```python
import jax
import jax.numpy as jnp
from jax import lax
from jax.sharding import PartitionSpec as P

HEADS = 64
NOPE = 128
ROPE = 64
LATENT = 512
RANK = 64
D = 3584
EH = 1024
TOPK = 8


masked_score = -1e30


def from_root(block, axis, holder):
    block = jnp.where(lax.axis_index(axis) == holder, block, jnp.zeros_like(block))
    return lax.psum(block, axis)


def attend(query_full, kv_cache, cache_lengths):
    scaling = 1.0 / (NOPE + ROPE) ** 0.5
    scores = (
        jnp.einsum("bhc,btc->bht", query_full, kv_cache, preferred_element_type=jnp.float32)
        * scaling
    )
    positions = lax.broadcasted_iota(jnp.int32, scores.shape, 2)
    valid_mask = positions < cache_lengths[:, None, None]
    scores = jnp.where(valid_mask, scores, masked_score)
    highest = jnp.max(scores, axis=2, keepdims=True)
    exponent = jnp.where(valid_mask, jnp.exp(scores - highest), 0.0)
    weights = (exponent / jnp.sum(exponent, axis=2, keepdims=True)).astype(jnp.bfloat16)
    latent = jnp.einsum(
        "bht,btl->bhl", weights, kv_cache[:, :, :LATENT], preferred_element_type=jnp.float32
    )
    return latent.astype(jnp.bfloat16)


def on_device(
    query_nope,
    query_rope,
    query_compressed,
    kv_cache,
    cache_lengths,
    key_base,
    query_down,
    query_rise,
    key_down,
    key_rise,
    moe_input,
    expert_ids,
    route_weights,
    expert_gate_up,
):
    adapter = (
        from_root(query_down, "rep", 0),
        from_root(query_rise, "rep", 0),
        from_root(key_down, "rep", 0),
        from_root(key_rise, "rep", 0),
    )
    query_down, query_rise, key_down, key_rise = [factor[0] for factor in adapter]
    row_count = moe_input.shape[0]
    query_low = jnp.dot(query_compressed, query_down, preferred_element_type=jnp.float32).astype(
        jnp.bfloat16
    )
    query_heads = (
        query_nope.astype(jnp.float32)
        + jnp.dot(query_low, query_rise, preferred_element_type=jnp.float32)
    ).astype(jnp.bfloat16)
    query_heads = query_heads.reshape(row_count, HEADS, NOPE)
    rise_heads = key_rise.reshape(RANK, HEADS, NOPE)
    low_rank = jnp.einsum("rhn,rl->hnl", rise_heads, key_down, preferred_element_type=jnp.float32)
    key_proj = lax.all_gather(key_base, "rep", axis=0, tiled=True).astype(jnp.float32) + low_rank
    query_latent = jnp.einsum(
        "ihn,hnl->ihl", query_heads.astype(jnp.float32), key_proj, precision=lax.Precision.HIGHEST
    ).astype(jnp.bfloat16)
    query_full = jnp.concatenate([query_latent, query_rope.reshape(row_count, HEADS, ROPE)], axis=2)
    attended = attend(query_full, kv_cache, cache_lengths).reshape(row_count, HEADS * LATENT)
    expert_total = lax.axis_size("rep") * lax.axis_size("ep")
    capacity = max(3, 2 * ((row_count * TOPK + expert_total - 1) // expert_total))
    flat_ids = expert_ids.reshape(-1)
    onehot = (flat_ids[:, None] == lax.broadcasted_iota(jnp.int32, (1, expert_total), 1)).astype(
        jnp.int32
    )
    earlier = jnp.cumsum(onehot, axis=0) - onehot
    slot_index = jnp.sum(earlier * onehot, axis=1)
    position = flat_ids * capacity + slot_index
    entry_rows = jnp.repeat(moe_input, TOPK, axis=0)
    outgoing = jnp.zeros((expert_total * capacity, D), jnp.bfloat16).at[position].set(entry_rows)
    expert_matrix = expert_gate_up[0]
    arrived = lax.all_to_all(
        outgoing.reshape(expert_total, capacity, D),
        ("rep", "ep"),
        split_axis=0,
        concat_axis=0,
        tiled=True,
    )
    shape_head = arrived.shape[:-1]
    gate_up = jnp.dot(arrived.reshape(-1, D), expert_matrix, preferred_element_type=jnp.float32)
    activation = (jax.nn.silu(gate_up[:, :EH]) * gate_up[:, EH:]).astype(jnp.bfloat16)
    returned = lax.all_to_all(
        activation.reshape(shape_head + (EH,)),
        ("rep", "ep"),
        split_axis=0,
        concat_axis=0,
        tiled=True,
    )
    results = returned.reshape(expert_total * capacity, EH)[position]
    scaled = route_weights.reshape(-1, 1) * results.astype(jnp.float32)
    expert_hidden = scaled.astype(jnp.bfloat16).reshape(row_count, TOPK * EH)
    return (attended, expert_hidden)


def solution(mesh):
    return jax.shard_map(
        on_device,
        mesh=mesh,
        in_specs=(
            P(("rep", "ep"), None),
            P(("rep", "ep"), None),
            P(("rep", "ep"), None),
            P(("rep", "ep"), None, None),
            P(("rep", "ep")),
            P("rep", None, None),
            P("rep", None, None),
            P("rep", None, None),
            P("rep", None, None),
            P("rep", None, None),
            P(("rep", "ep"), None),
            P(("rep", "ep"), None),
            P(("rep", "ep"), None),
            P(("rep", "ep"), None, None),
        ),
        out_specs=(P(("rep", "ep"), None), P(("rep", "ep"), None)),
        check_vma=False,
    )
```

profile of v0, /device:TPU:1, one launch (start us, length us, event | category | flops | bytes accessed | tf_op | source)
XLA Modules:
  0.0 256.7 jit_solution(4968389485092543814)
XLA Ops:
  7.2 1.4 select_bitcast_fusion.1
  8.6 0.3 copy.35
  8.9 1.6 copy.27
  10.6 1.1 select_bitcast_fusion
  11.7 0.7 select_bitcast_fusion.2
  12.4 0.6 select_bitcast_fusion.3
  13.1 0.7 all-gather.2.cloned.1.call-update
  14.1 0.2 reduce_window_sum.11
  14.4 0.2 select_reduce_fusion
  14.6 2.8 %scatter_custom_fusion = bf16[384,3584]{1,0:T(8,128)(2,1)S(1)} fusion(s32[128]{0:T(128)S(1)} %fusion.35, bf16[]{:T(256)} %constant.14.clone.1, bf16[16,3584]{1,0:T(8,128)(2,1)S(1)} %copy-done), kind=kCustom, calls=%fused_computation.17 | custom fusion | bytes 2867202 | tf_op jit(solution)/shard_map/scatter | solution.py:92
  17.5 4.1 %reshape.74 = bf16[128,3,3584]{2,1,0:T(4,128)(2,1)} reshape(bf16[384,3584]{1,0:T(8,128)(2,1)S(1)} %scatter_custom_fusion) | data formatting | bytes 5505024 | tf_op jit(solution)/shard_map/reshape | solution.py:95
  21.6 11.9 %all-to-all-start = ((bf16[128,3,3584]{2,1,0:T(4,128)(2,1)}), bf16[128,3,3584]{2,1,0:T(4,128)(2,1)}, u32[]{:S(2)}, u32[]{:S(2)}) async-start(bf16[128,3,3584]{2,1,0:T(4,128)(2,1)} %reshape.74), calls=%async_computation | async-start | bytes 7340032 | tf_op jit(solution)/shard_map/all_to_all | solution.py:94
  33.5 0.2 reshape.71
  33.8 0.9 copy.29
  34.8 0.3 copy.37
  35.2 69.0 %all-to-all-done = bf16[128,3,3584]{2,1,0:T(4,128)(2,1)} async-done(((bf16[128,3,3584]{2,1,0:T(4,128)(2,1)}), bf16[128,3,3584]{2,1,0:T(4,128)(2,1)}, u32[]{:S(2)}, u32[]{:S(2)}) %all-to-all-start) | async-done | bytes 2752544 | tf_op jit(solution)/shard_map/all_to_all | solution.py:94
  104.2 5.6 %reshape.75 = bf16[384,3584]{1,0:T(8,128)(2,1)S(1)} reshape(bf16[128,3,3584]{2,1,0:T(4,128)(2,1)} %all-to-all-done) | data formatting | bytes 5505024 | tf_op jit(solution)/shard_map/reshape | solution.py:102
  109.9 9.1 %fusion.4 = f32[384,2048]{1,0:T(8,128)S(1)} fusion(bf16[384,3584]{1,0:T(8,128)(2,1)S(1)} %reshape.75, bf16[1,3584,2048]{2,1,0:T(8,128)(2,1)} %param.27), kind=kOutput, calls=%fused_computation.6 | convolution fusion | flops 5637144576 | bytes 20578304 | tf_op jit(solution)/shard_map/dot_general | solution.py:102
  119.0 0.5 fusion.9
  119.5 1.3 reshape.76
  120.8 6.0 %all-to-all-start.1 = ((bf16[128,3,1024]{2,1,0:T(4,128)(2,1)}), bf16[128,3,1024]{2,1,0:T(4,128)(2,1)S(1)}, u32[]{:S(2)}, u32[]{:S(2)}) async-start(bf16[128,3,1024]{2,1,0:T(4,128)(2,1)} %reshape.76), calls=%async_computation.1 | async-start | bytes 2097152 | tf_op jit(solution)/shard_map/all_to_all | solution.py:104
  126.9 1.9 fusion.26
  128.8 11.5 %fusion.32 = f32[64,128,512]{2,1,0:T(8,128)} fusion(bf16[64,64,128]{2,0,1:T(8,128)(2,1)} %get-tuple-element.2, bf16[64,512]{1,0:T(8,128)(2,1)} %get-tuple-element.3), kind=kOutput, calls=%fused_computation.39 | convolution fusion | flops 536870912 | bytes 17891328 | tf_op jit(solution)/shard_map/rhn,rl->hnl/dot_general | solution.py:75
  140.2 9.3 %all-to-all-done.1 = bf16[128,3,1024]{2,1,0:T(4,128)(2,1)S(1)} async-done(((bf16[128,3,1024]{2,1,0:T(4,128)(2,1)}), bf16[128,3,1024]{2,1,0:T(4,128)(2,1)S(1)}, u32[]{:S(2)}, u32[]{:S(2)}) %all-to-all-start.1) | async-done | bytes 786464 | tf_op jit(solution)/shard_map/all_to_all | solution.py:104
  149.5 0.7 reshape.77
  150.2 0.9 gather_fusion
  151.2 0.8 multiply_convert_fusion
  152.0 78.2 %all-gather.2.cloned.1.call-done = bf16[64,128,512]{2,1,0:T(8,128)(2,1)} async-done(((bf16[32,128,512]{2,1,0:T(8,128)(2,1)}), bf16[64,128,512]{2,1,0:T(8,128)(2,1)}) %all-gather.2.cloned.1.call-update) | async-done | bytes 8388624 | tf_op jit(solution)/shard_map/all_gather | solution.py:76
  230.1 11.4 %fusion.19 = bf16[16,64,512]{2,0,1:T(8,128)(2,1)S(1)} fusion(f32[64,128,512]{2,1,0:T(8,128)} %fusion.32, bf16[64,128,512]{2,1,0:T(8,128)(2,1)} %all-gather.2.cloned.1.call-done, bf16[2,64,8,128]{3,2,1,0:T(8,128)(2,1)S(1)} %fusion.26), kind=kOutput, calls=%fused_computation.19 | convolution fusion | flops 814219264 | bytes 26476544 | tf_op jit(solution)/shard_map/ihn,hnl->ihl/dot_general | solution.py:77
  241.7 3.9 %fusion.36 = (f32[16,64]{1,0:T(8,128)S(1)}, f32[16,64,192]{2,1,0:T(8,128)S(1)}) fusion(s32[16]{0:T(128)S(1)} %copy-done.11, bf16[16,192,576]{2,1,0:T(8,128)(2,1)} %param.17, bf16[16,64,576]{2,0,1:T(8,128)(2,1)S(1)} %pad_maximum_fusion), kind=kOutput, calls=%fused_computation.50 | convolution fusion | flops 227868864 | bytes 5509184 | tf_op jit(solution)/shard_map/sub | solution.py:34
  245.6 2.7 %fusion.11 = bf16[16,64,512]{2,1,0:T(8,128)(2,1)S(1)} fusion(bf16[16,192,576]{2,1,0:T(8,128)(2,1)} %param.17, f32[16,64,192]{2,1,0:T(8,128)S(1)} %get-tuple-element.7, f32[16,64]{1,0:T(8,128)S(1)} %get-tuple-element.6), kind=kOutput, calls=%fused_computation.15 | convolution fusion | flops 202244096 | bytes 4984832 | tf_op jit(solution)/shard_map/bht,btl->bhl/dot_general | solution.py:36
  248.3 1.5 copy.36
  (40 shorter events, 1.0 us)
Async XLA Ops:
  7.2 7.5 %copy-start = (bf16[16,3584]{1,0:T(8,128)(2,1)S(1)}, bf16[16,3584]{1,0:T(8,128)(2,1)}, u32[]{:S(2)}) copy-start(bf16[16,3584]{1,0:T(8,128)(2,1)} %param.24) | copy-start | bytes 344068
  7.2 119.7 %all-reduce.3.cloned.1.call-start = ((), (), s32[]{:S(2)}) async-start(), calls=%async_computation.3 | async-start | bytes 4718592 | tf_op jit(solution)/shard_map/psum | solution.py:21
  7.2 3.4 %copy-start.2 = (bf16[1,64,8192]{2,1,0:T(8,128)(2,1)S(1)}, bf16[1,64,8192]{2,1,0:T(8,128)(2,1)}, u32[]{:S(2)}) copy-start(bf16[1,64,8192]{2,1,0:T(8,128)(2,1)} %param.21) | copy-start | bytes 3145732
  8.6 3.1 %copy-start.5 = (bf16[1,1536,64]{1,2,0:T(8,128)(2,1)S(1)}, bf16[1,1536,64]{1,2,0:T(8,128)(2,1)}, u32[]{:S(2)}) copy-start(bf16[1,1536,64]{1,2,0:T(8,128)(2,1)} %param.20) | copy-start | bytes 589828
  8.9 3.5 %copy-start.7 = (bf16[1,64,512]{2,1,0:T(8,128)(2,1)S(1)}, bf16[1,64,512]{2,1,0:T(8,128)(2,1)}, u32[]{:S(2)}) copy-start(bf16[1,64,512]{2,1,0:T(8,128)(2,1)} %param.22) | copy-start | bytes 196612
  13.1 0.8 copy-start.9
  13.1 217.0 %all-gather.2.cloned.1.call-start = ((), (), s32[]{:S(2)}) async-start(), calls=%async_computation.2 | async-start | bytes 12582912 | tf_op jit(solution)/shard_map/all_gather | solution.py:76
  21.6 11.9 %copy-start.6 = (bf16[16,4096]{1,0:T(8,128)(2,1)S(1)}, bf16[16,4096]{1,0:T(8,128)(2,1)}, u32[]{:S(2)}) copy-start(bf16[16,4096]{1,0:T(8,128)(2,1)} %param.15) | copy-start | bytes 393220
  21.6 13.1 %copy-start.10 = (f32[16,8]{0,1:T(8,128)S(1)}, f32[16,8]{0,1:T(8,128)}, u32[]{:S(2)}) copy-start(f32[16,8]{0,1:T(8,128)} %param.26) | copy-start | bytes 1540
  21.6 82.6 %all-to-all-start = ((bf16[128,3,3584]{2,1,0:T(4,128)(2,1)}), bf16[128,3,3584]{2,1,0:T(4,128)(2,1)}, u32[]{:S(2)}, u32[]{:S(2)}) async-start(bf16[128,3,3584]{2,1,0:T(4,128)(2,1)} %reshape.74), calls=%async_computation | async-start | bytes 7340032 | tf_op jit(solution)/shard_map/all_to_all | solution.py:94
  119.5 7.4 %copy-start.4 = (bf16[16,8192]{1,0:T(8,128)(2,1)S(1)}, bf16[16,8192]{1,0:T(8,128)(2,1)}, u32[]{:S(2)}) copy-start(bf16[16,8192]{1,0:T(8,128)(2,1)} %param.14) | copy-start | bytes 786436
  119.5 7.4 %copy-start.8 = (bf16[16,1536]{1,0:T(8,128)(2,1)S(1)}, bf16[16,1536]{1,0:T(8,128)(2,1)}, u32[]{:S(2)}) copy-start(bf16[16,1536]{1,0:T(8,128)(2,1)} %param.16) | copy-start | bytes 147460
  120.8 28.7 %all-to-all-start.1 = ((bf16[128,3,1024]{2,1,0:T(4,128)(2,1)}), bf16[128,3,1024]{2,1,0:T(4,128)(2,1)S(1)}, u32[]{:S(2)}, u32[]{:S(2)}) async-start(bf16[128,3,1024]{2,1,0:T(4,128)(2,1)} %reshape.76), calls=%async_computation.1 | async-start | bytes 2097152 | tf_op jit(solution)/shard_map/all_to_all | solution.py:104
  152.0 89.6 %copy-start.3 = (bf16[16,64,64]{2,0,1:T(8,128)(2,1)S(1)}, bf16[16,64,64]{2,0,1:T(8,128)(2,1)}, u32[]{:S(2)}) copy-start(bf16[16,64,64]{2,0,1:T(8,128)(2,1)} %copy.29) | copy-start | bytes 393220
  152.0 89.7 %copy-start.11 = (s32[16]{0:T(128)S(1)}, s32[16]{0:T(128)}, u32[]{:S(2)}) copy-start(s32[16]{0:T(128)} %param.18) | copy-start | bytes 196
  245.6 4.3 %copy-start.1 = (bf16[16,3584]{1,0:T(8,128)(2,1)S(1)}, bf16[16,3584]{1,0:T(8,128)(2,1)}, u32[]{:S(2)}) copy-start(bf16[16,3584]{1,0:T(8,128)(2,1)} %param.24) | copy-start | bytes 344068
Sparse Core Ops, SparseCore 0:
  13.2 104.5 all-reduce.2
  119.5 110.5 all-gather.1
where the time goes:
time: 257 us
  waiting for transfers between devices  157 us (61%)
  matrix products  40.4 us (16%)
  local copies, waits for them, and re-layouts  21 us (8%)
  starting transfers between devices  18 us (7%)
  between operations  14.3 us (6%)
  other arithmetic  5.66 us (2%)
    all_gather x1, waiting for transfers between devices, on_device(): lax.all_gather(key_base, 'rep', axis=0, tiled=True).astype(jnp.float32)  78.2 us
    all_to_all x1, waiting for transfers between devices, on_device(): lax.all_to_all(outgoing.reshape(expert_total, capacity, D), ('rep', 'ep')...  69 us
    all_to_all x1, starting transfers between devices, on_device(): lax.all_to_all(outgoing.reshape(expert_total, capacity, D), ('rep', 'ep')...  11.9 us
    dot_general x1, matrix products, on_device(): jnp.einsum('rhn,rl->hnl', rise_heads, key_down, preferred_element_type=jn...  11.5 us
    dot_general x1, matrix products, on_device(): jnp.einsum('ihn,hnl->ihl', query_heads.astype(jnp.float32), key_proj, pre...  11.4 us
    all_to_all x1, waiting for transfers between devices, on_device(): lax.all_to_all(activation.reshape(shape_head + (EH,)), ('rep', 'ep'), spl...  9.34 us
    dot_general x1, matrix products, on_device(): jnp.dot(arrived.reshape(-1, D), expert_matrix, preferred_element_type=jnp...  9.12 us
    all_to_all x1, starting transfers between devices, on_device(): lax.all_to_all(activation.reshape(shape_head + (EH,)), ('rep', 'ep'), spl...  6.04 us
  transfers between devices with their start and end apart: 4, of which 3 were waited for; matrix products, arithmetic and copies ran while one was open for 16% of the time, Pallas kernels for 0%

commit v1 on v0

v1 whole, which is shorter than its diff:
```python
import functools

import jax
import jax.numpy as jnp
from jax import lax
from jax.experimental import pallas as pl
from jax.experimental.pallas import tpu as pltpu
from jax.sharding import PartitionSpec as P

HEADS = 64
NOPE = 128
ROPE = 64
LATENT = 512
RANK = 64
QLORA = 1536
D = 3584
EH = 1024
TOPK = 8
ROWS = 16
LEN = 192
EXPERTS = 128
HALF = HEADS // 2
HCOLS = HALF * NOPE
GROUP = 8
PATH_COLS = HCOLS // 2
QUARTER = RANK // 4
COMP_AT = PATH_COLS
RISE_Q_AT = COMP_AT + QLORA
RISE_K_AT = RISE_Q_AT + HCOLS
DOWN_K_AT = RISE_K_AT + HCOLS
DOWN_Q_AT = DOWN_K_AT + LATENT
PAYLOAD = DOWN_Q_AT + QLORA
AXES = ("rep", "ep")
MIB = 1 << 20

f32 = jnp.float32
bf16 = jnp.bfloat16


def contract(a, b, dims):
    return lax.dot_general(a, b, (dims, ((), ())), preferred_element_type=f32)


def vmem():
    return pl.BlockSpec(memory_space=pltpu.VMEM)


def in_hbm(x):
    return pltpu.with_memory_space_constraint(x, pltpu.HBM)


def params(mib, **more):
    return pltpu.CompilerParams(vmem_limit_bytes=mib * MIB, **more)


def cost(flops, moved, exps=0):
    return pl.CostEstimate(flops=flops, bytes_accessed=moved, transcendentals=exps)


def named_and_rank(ids, slots, shift):
    expert = lax.broadcasted_iota(jnp.int32, (slots, ROWS), 0)
    if shift:
        expert = lax.shift_right_logical(expert, shift)
    named = jnp.zeros((slots, ROWS), f32)
    for c in range(TOPK):
        named = jnp.where(ids[c : c + 1, :] == expert, 1.0, named)
    above = lax.broadcasted_iota(jnp.int32, (ROWS, ROWS), 0) < lax.broadcasted_iota(
        jnp.int32, (ROWS, ROWS), 1
    )
    rank = contract(named.astype(bf16), above.astype(bf16), ((1,), (0,)))
    return named, rank


def slot_masks(ids):
    named, rank = named_and_rank(ids, 2 * EXPERTS, 1)
    slot = lax.broadcasted_iota(jnp.int32, (2 * EXPERTS, ROWS), 0) & 1
    mask_a = jnp.where(rank == slot.astype(f32), named, 0.0)
    named, rank = named_and_rank(ids, EXPERTS, 0)
    mask_b = jnp.where(rank == 2.0, named, 0.0)
    return mask_a, mask_b


PIECE = 512
PIECES = D // PIECE
TAKEN = (1, 1, 2, 2, 1)
SPAN = PIECE + PIECE // 2
TILE = 256
TILES = EH // TILE
STRIDE = TILE + TILE // 2


def payload_kernel(place_ref, *refs):
    widths = (PATH_COLS, QLORA, HCOLS, HCOLS, LATENT, QLORA)
    for path in range(2):
        at = 0
        for k, width in enumerate(widths):
            refs[12 + path][:, at : at + width] = refs[6 * path + k][...]
            at += width


def payloads(place, nope, comp, rise_q, rise_k, down_k, down_q):
    specs = []
    for path in range(2):
        quarter = lambda column, path=path: lambda _, p: (p[1] * 2 + path, column)
        specs += [
            pl.BlockSpec((ROWS, PATH_COLS), lambda _, p, path=path: (0, (1 - p[0]) * 2 + path)),
            pl.BlockSpec((ROWS, QLORA), lambda _, p: (0, 0)),
            pl.BlockSpec((QUARTER, HCOLS), quarter(1)),
            pl.BlockSpec((QUARTER, HCOLS), quarter(1)),
            pl.BlockSpec((QUARTER, LATENT), quarter(0)),
            pl.BlockSpec((QUARTER, QLORA), quarter(0)),
        ]
    given = tuple(map(in_hbm, (nope, comp, rise_q, rise_k, down_k, down_q)))
    return pl.pallas_call(
        payload_kernel,
        out_shape=(
            jax.ShapeDtypeStruct((ROWS, PAYLOAD), bf16),
            jax.ShapeDtypeStruct((ROWS, PAYLOAD), bf16),
        ),
        grid_spec=pltpu.PrefetchScalarGridSpec(
            num_scalar_prefetch=1,
            grid=(1,),
            in_specs=specs,
            out_specs=(pl.BlockSpec((ROWS, PAYLOAD), lambda _, p: (0, 0)),) * 2,
        ),
        compiler_params=params(16),
        cost_estimate=cost(1 << 10, 1 << 20),
        name="payloads",
    )(place, *given, *given)


def pack_kernel(ids_ref, x_ref, o_ref, packed_ref, sent):
    mask_a, mask_b = slot_masks(ids_ref[...])
    mask_a, mask_b = mask_a.astype(bf16), mask_b.astype(bf16)
    copies = []
    for g in range(PIECES):
        x = x_ref[:, g * PIECE : (g + 1) * PIECE]
        at = g * SPAN
        rows = contract(mask_a, x, ((1,), (0,))).astype(bf16)
        packed_ref[:, :, at : at + PIECE] = rows.reshape(EXPERTS, 2, PIECE)
        rows = contract(mask_b, x, ((1,), (0,))).astype(bf16)
        packed_ref[:, :, at + PIECE : at + SPAN] = rows.reshape(EXPERTS, 2, PIECE // 2)
        lanes = pl.ds(at, SPAN)
        copy = pltpu.make_async_copy(
            packed_ref.at[:, :, lanes], o_ref.at[:, :, lanes], sent.at[g]
        )
        copy.start()
        copies.append(copy)
    for copy in copies:
        copy.wait()


def pack(ids, x):
    shape = (EXPERTS, 2, PIECES * SPAN)
    return pl.pallas_call(
        pack_kernel,
        out_shape=pltpu.HBM(shape, bf16),
        in_specs=[vmem(), vmem()],
        out_specs=pl.BlockSpec(memory_space=pltpu.HBM),
        scratch_shapes=[pltpu.VMEM(shape, bf16), pltpu.SemaphoreType.DMA((PIECES,))],
        compiler_params=params(16),
        cost_estimate=cost(2 * 384 * ROWS * D, 3 * MIB),
        name="pack_rows",
    )(ids, x)


def expert_kernel(x_ref, w_ref, o_ref, xs_ref, held_ref, sum_ref, came):
    rows, wide = 3 * EXPERTS, 2 * TILE
    copies = []
    for g in range(PIECES):
        part = pl.ds(g * PIECE, PIECE)
        copy = pltpu.make_async_copy(w_ref.at[0, part, :], held_ref.at[part, :], came.at[g])
        copy.start()
        copies.append(copy)
    for g in range(PIECES):
        at, to = g * SPAN, slice(g * PIECE, (g + 1) * PIECE)
        xs_ref[: 2 * EXPERTS, to] = x_ref[:, :, at : at + PIECE].reshape(2 * EXPERTS, PIECE)
        xs_ref[2 * EXPERTS :, to] = x_ref[:, :, at + PIECE : at + SPAN].reshape(EXPERTS, PIECE)
    done = 0
    for take in TAKEN[:-1]:
        for g in range(done, done + take):
            copies[g].wait()
        part = slice(done * PIECE, (done + take) * PIECE)
        for n in range(2 * EH // wide):
            to = slice(n * wide, (n + 1) * wide)
            term = contract(xs_ref[:, part], held_ref[part, to], ((1,), (0,)))
            sum_ref[:, to] = term if done == 0 else sum_ref[:, to] + term
        done += take
    for g in range(done, PIECES):
        copies[g].wait()
    part = slice(done * PIECE, D)
    for n in range(TILES):
        both = []
        for k in range(2):
            to = slice(k * EH + n * TILE, k * EH + (n + 1) * TILE)
            term = contract(xs_ref[:, part], held_ref[part, to], ((1,), (0,)))
            both.append(sum_ref[:, to] + term)
        gate, up = both
        act = (gate / (1.0 + jnp.exp(-gate)) * up).astype(bf16)
        at = n * STRIDE
        o_ref[:, :, at : at + TILE] = act[: 2 * EXPERTS].reshape(EXPERTS, 2, TILE)
        o_ref[:, :, at + TILE : at + STRIDE] = act[2 * EXPERTS :].reshape(EXPERTS, 2, TILE // 2)


def expert(x, w):
    rows = 3 * EXPERTS
    x = pltpu.with_memory_space_constraint(x, pltpu.VMEM)
    return pl.pallas_call(
        expert_kernel,
        out_shape=pltpu.HBM((EXPERTS, 2, TILES * STRIDE), bf16),
        in_specs=[vmem(), pl.BlockSpec(memory_space=pltpu.HBM)],
        out_specs=pl.BlockSpec((EXPERTS, 2, TILES * STRIDE), lambda: (0, 0, 0)),
        scratch_shapes=[
            pltpu.VMEM((rows, D), bf16),
            pltpu.VMEM((D, 2 * EH), bf16),
            pltpu.VMEM((rows, 2 * EH), f32),
            pltpu.SemaphoreType.DMA((PIECES,)),
        ],
        compiler_params=params(40),
        cost_estimate=cost(2 * rows * D * 2 * EH, 18 * MIB, rows * EH),
        name="expert_rows",
    )(x, in_hbm(w))


def unpack_kernel(ids_ref, weight_ref, back_ref, o_ref):
    ids = ids_ref[...]
    mask_a, mask_b = slot_masks(ids)
    slot_a = lax.shift_right_logical(
        lax.broadcasted_iota(jnp.int32, (2 * EXPERTS, ROWS), 0), 1
    )
    slot_b = lax.broadcasted_iota(jnp.int32, (EXPERTS, ROWS), 0)
    pick_a = [jnp.where(ids[c : c + 1, :] == slot_a, mask_a, 0.0) for c in range(TOPK)]
    pick_b = [jnp.where(ids[c : c + 1, :] == slot_b, mask_b, 0.0) for c in range(TOPK)]
    pick_a = jnp.concatenate(pick_a, axis=1).astype(bf16)
    pick_b = jnp.concatenate(pick_b, axis=1).astype(bf16)
    for n in range(TILES):
        at = n * STRIDE
        slots = back_ref[:, :, at : at + TILE].reshape(2 * EXPERTS, TILE)
        third = back_ref[:, :, at + TILE : at + STRIDE].reshape(EXPERTS, TILE)
        found = contract(pick_a, slots, ((0,), (0,))) + contract(pick_b, third, ((0,), (0,)))
        for c in range(TOPK):
            to = c * EH + n * TILE
            part = weight_ref[:, c : c + 1] * found[c * ROWS : (c + 1) * ROWS]
            o_ref[:, to : to + TILE] = part.astype(bf16)


def unpack(ids, weights, back):
    return pl.pallas_call(
        unpack_kernel,
        out_shape=jax.ShapeDtypeStruct((ROWS, TOPK * EH), bf16),
        in_specs=[vmem()] * 3,
        out_specs=vmem(),
        compiler_params=params(16),
        cost_estimate=cost(2 * 384 * EXPERTS * EH, 2 * MIB),
        name="unpack_rows",
    )(ids, weights, back)


def query_kernel(rep_ref, nope_ref, comp_ref, from_same_ref, from_cross_ref, other_ref, rise_q_ref,
                 rise_k_ref, down_k_ref, down_q_ref, base_ref, own_ref, same_ref, cross_ref,
                 guest_ref, low_ref, rq_ref, rk_ref, dk_ref, dq_ref):
    step = pl.program_id(0)

    @pl.when(step == 0)
    def _():
        @pl.when(rep_ref[0] == 0)
        def _():
            rq_ref[...] = rise_q_ref[...]
            rk_ref[...] = rise_k_ref[...]
            dk_ref[...] = down_k_ref[...]
            dq_ref[...] = down_q_ref[...]

        @pl.when(rep_ref[0] != 0)
        def _():
            for ref, at, width in (
                (rq_ref, RISE_Q_AT, HCOLS),
                (rk_ref, RISE_K_AT, HCOLS),
                (dk_ref, DOWN_K_AT, LATENT),
                (dq_ref, DOWN_Q_AT, QLORA),
            ):
                ref[:QUARTER] = from_same_ref[:, at : at + width]
                ref[QUARTER : 2 * QUARTER] = from_cross_ref[:, at : at + width]
                at -= RISE_Q_AT
                ref[2 * QUARTER :] = other_ref[:, at : at + width]

        guest_ref[:, :PATH_COLS] = from_same_ref[:, :PATH_COLS]
        guest_ref[:, PATH_COLS:] = from_cross_ref[:, :PATH_COLS]
        down = dq_ref[...]
        comp = (
            comp_ref[...],
            from_same_ref[:, COMP_AT : COMP_AT + QLORA],
            from_cross_ref[:, COMP_AT : COMP_AT + QLORA],
        )
        for k in range(3):
            low = contract(comp[k], down, ((1,), (1,)))
            low_ref[k * ROWS : (k + 1) * ROWS] = low.astype(bf16)

    cols = pl.ds(pl.multiple_of(step * GROUP * NOPE, GROUP * NOPE), GROUP * NOPE)
    path = lax.div(step, 2)
    guest = pl.ds(pl.multiple_of((1 + path) * ROWS, ROWS), ROWS)
    low = jnp.concatenate([low_ref[:ROWS], low_ref[guest]], axis=0)
    nope = jnp.concatenate([nope_ref[...], guest_ref[:, cols]], axis=0)
    delta = contract(low, rq_ref[:, cols], ((1,), (0,)))
    heads = (nope.astype(f32) + delta).astype(bf16)
    rise = rk_ref[:, cols]
    down = dk_ref[...]
    kept = []
    for h in range(GROUP):
        query = heads[:, h * NOPE : (h + 1) * NOPE]
        mixed = contract(query, rise[:, h * NOPE : (h + 1) * NOPE], ((1,), (1,)))
        high = mixed.astype(bf16)
        rest = (mixed - high.astype(f32)).astype(bf16)
        latent = (
            contract(query, base_ref[h], ((1,), (0,)))
            + contract(high, down, ((1,), (0,)))
            + contract(rest, down, ((1,), (0,)))
        )
        own_ref[h] = latent[:ROWS].astype(bf16)
        kept.append(latent[ROWS:].astype(bf16))

    @pl.when(path == 0)
    def _():
        for h in range(GROUP):
            same_ref[h] = kept[h]

    @pl.when(path != 0)
    def _():
        for h in range(GROUP):
            cross_ref[h] = kept[h]


def query_part(rep, nope, comp, from_same, from_cross, other, rise_q, rise_k, down_k, down_q, base):
    steps = HALF // GROUP
    block = (GROUP, ROWS, LATENT)
    return pl.pallas_call(
        query_kernel,
        out_shape=(
            jax.ShapeDtypeStruct((HALF, ROWS, LATENT), bf16),
            jax.ShapeDtypeStruct((HALF // 2, ROWS, LATENT), bf16),
            jax.ShapeDtypeStruct((HALF // 2, ROWS, LATENT), bf16),
        ),
        grid_spec=pltpu.PrefetchScalarGridSpec(
            num_scalar_prefetch=1,
            grid=(steps,),
            in_specs=[
                pl.BlockSpec((ROWS, GROUP * NOPE), lambda g, r: (0, r[0] * steps + g)),
                pl.BlockSpec((ROWS, QLORA), lambda g, r: (0, 0)),
                pl.BlockSpec((ROWS, PAYLOAD), lambda g, r: (0, 0)),
                pl.BlockSpec((ROWS, PAYLOAD), lambda g, r: (0, 0)),
                pl.BlockSpec((2 * QUARTER, PAYLOAD - RISE_Q_AT), lambda g, r: (0, 0)),
                pl.BlockSpec((RANK, HCOLS), lambda g, r: (0, 0)),
                pl.BlockSpec((RANK, HCOLS), lambda g, r: (0, 0)),
                pl.BlockSpec((RANK, LATENT), lambda g, r: (0, 0)),
                pl.BlockSpec((RANK, QLORA), lambda g, r: (0, 0)),
                pl.BlockSpec((GROUP, NOPE, LATENT), lambda g, r: (g, 0, 0)),
            ],
            out_specs=(
                pl.BlockSpec(block, lambda g, r: (g, 0, 0)),
                pl.BlockSpec(block, lambda g, r: (jnp.minimum(g, 1), 0, 0)),
                pl.BlockSpec(block, lambda g, r: (jnp.maximum(g - 2, 0), 0, 0)),
            ),
            scratch_shapes=[
                pltpu.VMEM((ROWS, HCOLS), bf16),
                pltpu.VMEM((3 * ROWS, RANK), bf16),
                pltpu.VMEM((RANK, HCOLS), bf16),
                pltpu.VMEM((RANK, HCOLS), bf16),
                pltpu.VMEM((RANK, LATENT), bf16),
                pltpu.VMEM((RANK, QLORA), bf16),
            ],
        ),
        compiler_params=params(24),
        cost_estimate=cost(20000000000, 1 << 10),
        name="query_latent",
    )(rep, in_hbm(nope), comp, from_same, from_cross, other, *map(in_hbm, (rise_q, rise_k, down_k, down_q, base)))


BATCH = 2
LANES = LATENT // 128


def attend_kernel(lengths_ref, rep_ref, own_ref, same_ref, cross_ref, rope_ref, kv_ref,
                  o_ref, query_ref, done_ref):
    step = pl.program_id(0)

    @pl.when(step == 0)
    def _():
        mine = rep_ref[0] * HALF
        other = HALF - mine
        for h in range(HALF):
            at = pl.multiple_of((mine + h) * ROWS, ROWS)
            value = own_ref[h].astype(f32)
            for j in range(LANES):
                query_ref[j, pl.ds(at, ROWS), :] = value[:, j * 128 : (j + 1) * 128]
        for k, ref in enumerate((same_ref, cross_ref)):
            for h in range(HALF // 2):
                at = pl.multiple_of((other + k * (HALF // 2) + h) * ROWS, ROWS)
                value = ref[h].astype(f32)
                for j in range(LANES):
                    query_ref[j, pl.ds(at, ROWS), :] = value[:, j * 128 : (j + 1) * 128]

    for b in range(BATCH):
        row = step * BATCH + b
        query = jnp.concatenate(
            [query_ref[j, pl.ds(row, HEADS, stride=ROWS), :] for j in range(LANES)], axis=1
        ).astype(bf16)
        kv = kv_ref[b]
        scores = contract(query, kv[:, :LATENT], ((1,), (1,))) + contract(
            rope_ref[b], kv[:, LATENT:], ((1,), (1,))
        )
        scores = scores * (1.0 / (NOPE + ROPE) ** 0.5)
        live = lax.broadcasted_iota(jnp.int32, scores.shape, 1) < lengths_ref[row]
        scores = jnp.where(live, scores, -1e30)
        highest = jnp.max(scores, axis=1, keepdims=True)
        exponent = jnp.where(live, jnp.exp(scores - highest), 0.0)
        weights = (exponent / jnp.sum(exponent, axis=1, keepdims=True)).astype(bf16)
        at = pl.multiple_of(row * HEADS, HEADS)
        latent = contract(weights, kv[:, :LATENT], ((1,), (0,)))
        for j in range(LANES):
            done_ref[j, pl.ds(at, HEADS), :] = latent[:, j * 128 : (j + 1) * 128]

    @pl.when(step == pl.num_programs(0) - 1)
    def _():
        for h in range(HEADS):
            for j in range(LANES):
                at = h * LATENT + j * 128
                o_ref[:, at : at + 128] = done_ref[
                    j, pl.ds(h, ROWS, stride=HEADS), :
                ].astype(bf16)


def attend(lengths, rep, own, same, cross, rope, kv):
    whole = lambda s, *_: (0, 0, 0)
    half = pl.BlockSpec((HALF // 2, ROWS, LATENT), whole)
    return pl.pallas_call(
        attend_kernel,
        out_shape=jax.ShapeDtypeStruct((ROWS, HEADS * LATENT), bf16),
        grid_spec=pltpu.PrefetchScalarGridSpec(
            num_scalar_prefetch=2,
            grid=(ROWS // BATCH,),
            in_specs=[
                pl.BlockSpec((HALF, ROWS, LATENT), whole),
                half,
                half,
                pl.BlockSpec((BATCH, HEADS, ROPE), lambda s, *_: (s, 0, 0)),
                pl.BlockSpec((BATCH, LEN, LATENT + ROPE), lambda s, *_: (s, 0, 0)),
            ],
            out_specs=pl.BlockSpec((ROWS, HEADS * LATENT), lambda s, *_: (0, 0)),
            scratch_shapes=[
                pltpu.VMEM((LANES, HEADS * ROWS, 128), f32),
                pltpu.VMEM((LANES, ROWS * HEADS, 128), f32),
            ],
        ),
        compiler_params=params(40),
        cost_estimate=cost(2 * ROWS * HEADS * LEN * 1088, 6 * MIB, ROWS * HEADS * LEN),
        name="attend_rows",
    )(lengths, rep, own, same, cross, rope, in_hbm(kv))


def on_device(
    query_nope,
    query_rope,
    query_compressed,
    kv_cache,
    cache_lengths,
    key_base,
    query_down,
    query_rise,
    key_down,
    key_rise,
    moe_input,
    expert_ids,
    route_weights,
    expert_gate_up,
):
    rep = lax.axis_index("rep")
    core = lax.axis_index("ep") % 2
    ep_size = lax.axis_size("ep")
    every = [(r, e) for r in range(2) for e in range(ep_size)]
    place = lambda r, e: r * ep_size + e
    to_same = [(place(r, e), place(1 - r, e)) for r, e in every]
    to_cross = [(place(r, e), place(1 - r, e ^ 2)) for r, e in every]
    to_core = [(e, e ^ 1) for e in range(ep_size)]

    factors = (query_rise[0], key_rise[0], key_down[0], query_down[0].T)
    same, cross = payloads(jnp.stack([rep, core]), query_nope, query_compressed, *factors)
    moe_input, same, cross = lax.optimization_barrier((moe_input, same, cross))
    leaving_rows = pack(expert_ids.T, moe_input)
    arrived_rows = lax.all_to_all(leaving_rows, AXES, 0, 0, tiled=True)

    from_same = lax.ppermute(same, AXES, to_same)
    from_cross = lax.ppermute(cross, AXES, to_cross)
    half = jnp.concatenate([from_same[:, RISE_Q_AT:], from_cross[:, RISE_Q_AT:]], axis=0)
    other = lax.ppermute(half, "ep", to_core)
    own, same, cross = query_part(
        rep.reshape(1), query_nope, query_compressed, from_same, from_cross, other, *factors, key_base
    )
    same = lax.ppermute(same, AXES, to_same)
    cross = lax.ppermute(cross, AXES, to_cross)
    arrived_rows, own = lax.optimization_barrier((arrived_rows, own))
    rope = query_rope.reshape(ROWS, HEADS, ROPE)
    activation = expert(arrived_rows, expert_gate_up)
    activation, same, cross = lax.optimization_barrier((activation, same, cross))
    back = lax.all_to_all(activation, AXES, 0, 0, tiled=True)
    attended = attend(cache_lengths, rep.reshape(1), own, same, cross, rope, kv_cache)
    expert_hidden = unpack(expert_ids.T, route_weights, back)
    return (attended, expert_hidden)


def solution(mesh):
    both = ("rep", "ep")
    return jax.shard_map(
        on_device,
        mesh=mesh,
        in_specs=(
            P(both, None),
            P(both, None),
            P(both, None),
            P(both, None, None),
            P(both),
            P("rep", None, None),
            P("rep", None, None),
            P("rep", None, None),
            P("rep", None, None),
            P("rep", None, None),
            P(both, None),
            P(both, None),
            P(both, None),
            P(both, None, None),
        ),
        out_specs=(P(both, None), P(both, None)),
        check_vma=False,
    )
```

time: 257 us -> 89.6 us (0.35)
  waiting for transfers between devices: 157 us -> 26.6 us
  matrix products: 40.4 us -> 0 us
  Pallas kernels: 0 us -> 36.4 us
  local copies, waits for them, and re-layouts: 21 us -> 3.44 us
  between operations: 14.3 us -> 0.78 us
  other arithmetic: 5.66 us -> 0.12 us
  starting transfers between devices: 18 us -> 21.6 us
    all_gather x1 -> x0, waiting for transfers between devices: 78.2 us -> none  [on_device(): lax.all_gather(key_base, 'rep', axis=0, tiled=True).astype(jnp.float32)]
    all_to_all x2, waiting for transfers between devices: 78.4 us -> 24.9 us  [the longest x1 22.4 us: on_device(): arrived_rows = lax.all_to_all(leaving_rows, AXES, 0, 0, tiled=True)]
    dot_general x5 -> x0, matrix products: 36.5 us -> none  [the longest x1 11.5 us: on_device(): jnp.einsum('rhn,rl->hnl', rise_heads, key_down, preferred_element_type=jn...]
    pallas_call x0 -> x6, Pallas kernels: none -> 36.4 us  [the longest x1 12.8 us: attend(): pl.pallas_call(attend_kernel, out_shape=jax.ShapeDtypeStruct((ROWS, HEADS...]
    reshape x6 -> x1, local copies, waits for them, and re-layouts: 12.8 us -> 1.18 us  [on_device(): rope = query_rope.reshape(ROWS, HEADS, ROPE)]
    ppermute x0 -> x5, starting transfers between devices: none -> 6.94 us  [the longest x1 3.31 us: on_device(): from_cross = lax.ppermute(cross, AXES, to_cross)]
    sub x1 -> x0, matrix products: 3.88 us -> none  [attend(): exponent = jnp.where(valid_mask, jnp.exp(scores - highest), 0.0)]
    all_to_all x2, starting transfers between devices: 17.9 us -> 14.6 us  [the longest x1 9.95 us: on_device(): arrived_rows = lax.all_to_all(leaving_rows, AXES, 0, 0, tiled=True)]
  transfers between devices with their start and end apart: 4 -> 7, of which waited for: 3 -> 3; matrix products, arithmetic and copies ran while one was open for 16% -> 3% of each run, Pallas kernels for 0% -> 36%
where the time goes in v1:
time: 89.6 us; the launch traced here: 89 us
  Pallas kernels  36.4 us (41%)
  waiting for transfers between devices  26.6 us (30%)
  starting transfers between devices  21.6 us (24%)
  local copies, waits for them, and re-layouts  3.44 us (4%)
    all_to_all x1, waiting for transfers between devices, on_device(): arrived_rows = lax.all_to_all(leaving_rows, AXES, 0, 0, tiled=True)  22.4 us
    pallas_call x1, Pallas kernels, attend(): pl.pallas_call(attend_kernel, out_shape=jax.ShapeDtypeStruct((ROWS, HEADS...  12.8 us
    all_to_all x1, starting transfers between devices, on_device(): arrived_rows = lax.all_to_all(leaving_rows, AXES, 0, 0, tiled=True)  9.95 us
    pallas_call x1, Pallas kernels, expert(): pl.pallas_call(expert_kernel, out_shape=pltpu.HBM((EXPERTS, 2, TILES * ST...  9.47 us
    pallas_call x1, Pallas kernels, query_part(): pl.pallas_call(query_kernel, out_shape=(jax.ShapeDtypeStruct((HALF, ROWS,...  7.47 us
    all_to_all x1, starting transfers between devices, on_device(): back = lax.all_to_all(activation, AXES, 0, 0, tiled=True)  4.7 us
    ppermute x1, starting transfers between devices, on_device(): from_cross = lax.ppermute(cross, AXES, to_cross)  3.31 us
    pallas_call x1, Pallas kernels, payloads(): pl.pallas_call(payload_kernel, out_shape=(jax.ShapeDtypeStruct((ROWS, PAY...  2.74 us
  transfers between devices with their start and end apart: 7, of which 3 were waited for; matrix products, arithmetic and copies ran while one was open for 3% of the time, Pallas kernels for 36%

profile of v1, /device:TPU:1, one launch (start us, length us, event | category | flops | bytes accessed | tf_op | source)
XLA Modules:
  0.0 89.0 jit_solution(13813079579272645728)
XLA Ops:
  0.6 0.0 copy-start.3
  0.6 0.0 copy-start.4
  0.7 0.1 pad_add_fusion.place_ref
  0.7 2.7 %payloads.1 = (bf16[16,13824]{1,0:T(8,128)(2,1)}, bf16[16,13824]{1,0:T(8,128)(2,1)}) custom-call(s32[2]{0:T(128)S(1)} %pad_add_fusion.place_ref, bf16[16,8192]{1,0:T(8,128)(2,1)} %nope_ref.1, bf16[16,1536]{1,0:T(8,128)(2,1)} %comp_ref.1, bf16[64,8192]{1,0:T(8,128)(2,1)} %bitcast.11, bf16[64,8192]{1,0:T(8,128)(2,1)} %bitcast.14, bf16[64,512]{1,0:T(8,128)(2,1)} %bitcast.20, ...), custom_call_target="tpu_custom_call" | custom-call | flops 1024 | bytes 1048576 | tf_op jit(solution)/shard_map/payloads/pallas_call | solution.py:114
  3.5 3.3 %collective-permute-start.1 = (bf16[16,13824]{1,0:T(8,128)(2,1)}, bf16[16,13824]{1,0:T(8,128)(2,1)S(1)}, u32[]{:S(2)}, u32[]{:S(2)}) collective-permute-start(bf16[16,13824]{1,0:T(8,128)(2,1)} %get-tuple-element.19), channel_id=1, source_target_pairs={{0,66},{1,67},{2,64},{3,65},{4,70},{5,71},{6,68},{7,69},{8,74},{9,... | collective-permute-start | bytes 1327112 | tf_op jit(solution)/shard_map/ppermute | solution.py:491
  6.8 0.0 collective-permute-start
  6.8 0.0 copy-done.3
  6.8 0.0 copy-done.4
  6.8 2.3 %pack_rows.1 = bf16[128,2,5376]{2,1,0:T(2,128)(2,1)} custom-call(s32[8,16]{1,0:T(8,128)S(1)} %bitcast.9, bf16[16,3584]{1,0:T(8,128)(2,1)S(1)} %copy-done.3), custom_call_target="tpu_custom_call" | custom-call | flops 44040192 | bytes 3145728 | tf_op jit(solution)/shard_map/pack_rows/pallas_call | solution.py:155
  9.1 0.0 copy-start.2
  9.1 9.9 %all-to-all-start = ((bf16[128,2,5376]{2,1,0:T(2,128)(2,1)}), bf16[128,2,5376]{2,1,0:T(2,128)(2,1)S(1)}, u32[]{:S(2)}, u32[]{:S(2)}) async-start(bf16[128,2,5376]{2,1,0:T(2,128)(2,1)} %pack_rows.1), calls=%async_computation | async-start | bytes 5505024 | tf_op jit(solution)/shard_map/all_to_all | solution.py:488
  19.1 0.0 collective-permute-done.1.from_cross_ref
  19.1 0.0 copy-start
  19.1 0.0 collective-permute-done.from_same_ref
  19.1 1.1 %slice.8 = bf16[16,10240]{1,0:T(8,128)(2,1)S(1)} slice(bf16[16,13824]{1,0:T(8,128)(2,1)} %collective-permute-done.from_same_ref), slice={[0:16], [3584:13824]} | slice | bytes 655360 | tf_op jit(solution)/shard_map/slice | solution.py:492
  20.3 1.1 %collective-permute-start.2 = (bf16[32,10240]{1,0:T(8,128)(2,1)S(1)}, bf16[32,10240]{1,0:T(8,128)(2,1)S(1)}, u32[]{:S(2)}, u32[]{:S(2)}) collective-permute-start(bf16[32,10240]{1,0:T(8,128)(2,1)S(1)} %pad_maximum_fusion), channel_id=1, source_target_pairs={{0,1},{1,0},{2,3},{3,2},{4,5},{5,4},{6,7},{7,6},{8,9},{9,8},{10,11... | collective-permute-start | bytes 1966088 | tf_op jit(solution)/shard_map/ppermute | solution.py:493
  21.5 1.7 %collective-permute-done.2.other_ref = bf16[32,10240]{1,0:T(8,128)(2,1)S(1)} collective-permute-done((bf16[32,10240]{1,0:T(8,128)(2,1)S(1)}, bf16[32,10240]{1,0:T(8,128)(2,1)S(1)}, u32[]{:S(2)}, u32[]{:S(2)}) %collective-permute-start.2) | collective-permute-done | bytes 655392 | tf_op jit(solution)/shard_map/ppermute | solution.py:493
  23.2 1.0 %copy-done.1 = bf16[16,13824]{1,0:T(8,128)(2,1)S(1)} copy-done((bf16[16,13824]{1,0:T(8,128)(2,1)S(1)}, bf16[16,13824]{1,0:T(8,128)(2,1)}, u32[]{:S(2)}) %copy-start.1) | copy-done | bytes 442392
  24.2 7.5 %query_latent.1 = (bf16[32,16,512]{2,1,0:T(8,128)(2,1)S(1)}, bf16[16,16,512]{2,1,0:T(8,128)(2,1)}, bf16[16,16,512]{2,1,0:T(8,128)(2,1)}) custom-call(s32[1]{0:T(128)} %bitcast.rep_ref, bf16[16,8192]{1,0:T(8,128)(2,1)} %nope_ref.1, bf16[16,1536]{1,0:T(8,128)(2,1)S(1)} %copy-done.2, bf16[16,13824]{1,0:T(8,128)(2,1)} %collective-permute-done.from_same_ref, ...), custom_call_target="tpu_custom_call" | custom-call | flops 20000000000 | bytes 1024 | tf_op jit(solution)/shard_map/query_latent/pallas_call | solution.py:335
  31.7 0.7 collective-permute-start.3
  32.4 1.8 %collective-permute-start.4 = (bf16[16,16,512]{2,1,0:T(8,128)(2,1)}, bf16[16,16,512]{2,1,0:T(8,128)(2,1)}, u32[]{:S(2)}, u32[]{:S(2)}) collective-permute-start(bf16[16,16,512]{2,1,0:T(8,128)(2,1)} %get-tuple-element.24), channel_id=1, source_target_pairs={{0,66},{1,67},{2,64},{3,65},{4,70},{5,71},{6,68},{7,69},{8,74},{9,... | collective-permute-start | bytes 786440 | tf_op jit(solution)/shard_map/ppermute | solution.py:498
  34.2 22.4 %all-to-all-done.x_ref = bf16[128,2,5376]{2,1,0:T(2,128)(2,1)S(1)} async-done(((bf16[128,2,5376]{2,1,0:T(2,128)(2,1)}), bf16[128,2,5376]{2,1,0:T(2,128)(2,1)S(1)}, u32[]{:S(2)}, u32[]{:S(2)}) %all-to-all-start) | async-done | bytes 2752544 | tf_op jit(solution)/shard_map/all_to_all | solution.py:488
  56.6 9.5 %expert_rows.1 = bf16[128,2,1536]{2,1,0:T(2,128)(2,1)} custom-call(bf16[128,2,5376]{2,1,0:T(2,128)(2,1)S(1)} %all-to-all-done.x_ref, bf16[1,3584,2048]{2,1,0:T(8,128)(2,1)} %w_ref.1), custom_call_target="tpu_custom_call" | custom-call | flops 5637144576 | bytes 18874368 | tf_op jit(solution)/shard_map/expert_rows/pallas_call | solution.py:208
  66.1 0.0 collective-permute-done.3.same_ref
  66.1 0.0 collective-permute-done.4.cross_ref
  66.1 4.7 %all-to-all-start.1 = ((bf16[128,2,1536]{2,1,0:T(2,128)(2,1)}), bf16[128,2,1536]{2,1,0:T(2,128)(2,1)S(1)}, u32[]{:S(2)}, u32[]{:S(2)}) async-start(bf16[128,2,1536]{2,1,0:T(2,128)(2,1)} %expert_rows.1), calls=%async_computation.1 | async-start | bytes 1572864 | tf_op jit(solution)/shard_map/all_to_all | solution.py:503
  70.8 1.2 %reshape.12.rope_ref = bf16[16,64,64]{2,1,0:T(8,128)(2,1)S(1)} reshape(bf16[16,4096]{1,0:T(8,128)(2,1)} %param.15) | data formatting | bytes 262144 | tf_op jit(solution)/shard_map/reshape | solution.py:500
  72.0 0.0 copy-done.6
  72.0 0.1 copy.16.weight_ref
  72.1 12.8 %attend_rows.1 = bf16[16,32768]{1,0:T(8,128)(2,1)} custom-call(s32[16]{0:T(128)S(1)} %copy-done.5, s32[1]{0:T(128)} %bitcast.rep_ref, bf16[32,16,512]{2,1,0:T(8,128)(2,1)S(1)} %get-tuple-element.21.own_ref, bf16[16,16,512]{2,1,0:T(8,128)(2,1)S(1)} %collective-permute-done.3.same_ref, bf16[16,16,512]{2,1,0:T(8,128)(2,1)} %collective-permute-done.4.cross_ref, ...), custom_call_target="tpu_custom_call" | custom-call | flops 427819008 | bytes 6291456 | tf_op jit(solution)/shard_map/attend_rows/pallas_call | solution.py:434
  84.8 2.5 %all-to-all-done.1.back_ref = bf16[128,2,1536]{2,1,0:T(2,128)(2,1)S(1)} async-done(((bf16[128,2,1536]{2,1,0:T(2,128)(2,1)}), bf16[128,2,1536]{2,1,0:T(2,128)(2,1)S(1)}, u32[]{:S(2)}, u32[]{:S(2)}) %all-to-all-start.1) | async-done | bytes 786464 | tf_op jit(solution)/shard_map/all_to_all | solution.py:503
  87.3 1.7 %unpack_rows.1 = bf16[16,8192]{1,0:T(8,128)(2,1)} custom-call(s32[8,16]{1,0:T(8,128)S(1)} %bitcast.10, f32[16,8]{1,0:T(8,128)S(1)} %copy.16.weight_ref, bf16[128,2,1536]{2,1,0:T(2,128)(2,1)S(1)} %all-to-all-done.1.back_ref), custom_call_target="tpu_custom_call" | custom-call | flops 100663296 | bytes 2097152 | tf_op jit(solution)/shard_map/unpack_rows/pallas_call | solution.py:248
  (8 shorter events, 0.1 us)
Async XLA Ops:
  0.6 6.2 %copy-start.3 = (bf16[16,3584]{1,0:T(8,128)(2,1)S(1)}, bf16[16,3584]{1,0:T(8,128)(2,1)}, u32[]{:S(2)}) copy-start(bf16[16,3584]{1,0:T(8,128)(2,1)} %x_ref) | copy-start | bytes 344068
  0.6 6.2 %copy-start.4 = (s32[16,8]{0,1:T(8,128)S(1)}, s32[16,8]{0,1:T(8,128)}, u32[]{:S(2)}) copy-start(s32[16,8]{0,1:T(8,128)} %param.25) | copy-start | bytes 1540
  3.5 15.6 %collective-permute-start.1 = (bf16[16,13824]{1,0:T(8,128)(2,1)}, bf16[16,13824]{1,0:T(8,128)(2,1)S(1)}, u32[]{:S(2)}, u32[]{:S(2)}) collective-permute-start(bf16[16,13824]{1,0:T(8,128)(2,1)} %get-tuple-element.19), channel_id=1, source_target_pairs={{0,66},{1,67},{2,64},{3,65},{4,70},{5,71},{6,68},{7,69},{8,74},{9,... | collective-permute-start | bytes 1327112 | tf_op jit(solution)/shard_map/ppermute | solution.py:491
  6.8 12.3 %collective-permute-start = (bf16[16,13824]{1,0:T(8,128)(2,1)}, bf16[16,13824]{1,0:T(8,128)(2,1)}, u32[]{:S(2)}, u32[]{:S(2)}) collective-permute-start(bf16[16,13824]{1,0:T(8,128)(2,1)} %get-tuple-element.18), channel_id=1, source_target_pairs={{0,64},{1,65},{2,66},{3,67},{4,68},{5,69},{6,70},{7,71},{8,72},{9,... | collective-permute-start | bytes 1327112 | tf_op jit(solution)/shard_map/ppermute | solution.py:490
  9.1 14.1 %copy-start.2 = (bf16[16,1536]{1,0:T(8,128)(2,1)S(1)}, bf16[16,1536]{1,0:T(8,128)(2,1)}, u32[]{:S(2)}) copy-start(bf16[16,1536]{1,0:T(8,128)(2,1)} %comp_ref.1) | copy-start | bytes 147460
  9.1 47.5 %all-to-all-start = ((bf16[128,2,5376]{2,1,0:T(2,128)(2,1)}), bf16[128,2,5376]{2,1,0:T(2,128)(2,1)S(1)}, u32[]{:S(2)}, u32[]{:S(2)}) async-start(bf16[128,2,5376]{2,1,0:T(2,128)(2,1)} %pack_rows.1), calls=%async_computation | async-start | bytes 5505024 | tf_op jit(solution)/shard_map/all_to_all | solution.py:488
  19.1 2.4 %copy-start = (bf16[16,13824]{1,0:T(8,128)(2,1)}, bf16[16,13824]{1,0:T(8,128)(2,1)S(1)}, u32[]{:S(2)}) copy-start(bf16[16,13824]{1,0:T(8,128)(2,1)S(1)} %collective-permute-done.1.from_cross_ref) | copy-start | bytes 1327108
  20.3 2.9 %collective-permute-start.2 = (bf16[32,10240]{1,0:T(8,128)(2,1)S(1)}, bf16[32,10240]{1,0:T(8,128)(2,1)S(1)}, u32[]{:S(2)}, u32[]{:S(2)}) collective-permute-start(bf16[32,10240]{1,0:T(8,128)(2,1)S(1)} %pad_maximum_fusion), channel_id=1, source_target_pairs={{0,1},{1,0},{2,3},{3,2},{4,5},{5,4},{6,7},{7,6},{8,9},{9,8},{10,11... | collective-permute-start | bytes 1966088 | tf_op jit(solution)/shard_map/ppermute | solution.py:493
  23.2 1.0 %copy-start.1 = (bf16[16,13824]{1,0:T(8,128)(2,1)S(1)}, bf16[16,13824]{1,0:T(8,128)(2,1)}, u32[]{:S(2)}) copy-start(bf16[16,13824]{1,0:T(8,128)(2,1)} %copy-done) | copy-start | bytes 1327108
  31.7 34.4 %collective-permute-start.3 = (bf16[16,16,512]{2,1,0:T(8,128)(2,1)}, bf16[16,16,512]{2,1,0:T(8,128)(2,1)S(1)}, u32[]{:S(2)}, u32[]{:S(2)}) collective-permute-start(bf16[16,16,512]{2,1,0:T(8,128)(2,1)} %get-tuple-element.23), channel_id=1, source_target_pairs={{0,64},{1,65},{2,66},{3,67},{4,68},{5,69},{6,70},{7,71},{8,72},{9,... | collective-permute-start | bytes 786440 | tf_op jit(solution)/shard_map/ppermute | solution.py:497
  32.4 33.7 %collective-permute-start.4 = (bf16[16,16,512]{2,1,0:T(8,128)(2,1)}, bf16[16,16,512]{2,1,0:T(8,128)(2,1)}, u32[]{:S(2)}, u32[]{:S(2)}) collective-permute-start(bf16[16,16,512]{2,1,0:T(8,128)(2,1)} %get-tuple-element.24), channel_id=1, source_target_pairs={{0,66},{1,67},{2,64},{3,65},{4,70},{5,71},{6,68},{7,69},{8,74},{9,... | collective-permute-start | bytes 786440 | tf_op jit(solution)/shard_map/ppermute | solution.py:498
  56.6 15.4 %copy-start.6 = (f32[16,8]{0,1:T(8,128)S(1)}, f32[16,8]{0,1:T(8,128)}, u32[]{:S(2)}) copy-start(f32[16,8]{0,1:T(8,128)} %param.26) | copy-start | bytes 1540
  56.6 15.5 %copy-start.5 = (s32[16]{0:T(128)S(1)}, s32[16]{0:T(128)}, u32[]{:S(2)}) copy-start(s32[16]{0:T(128)} %lengths_ref.1) | copy-start | bytes 196
  66.1 21.2 %all-to-all-start.1 = ((bf16[128,2,1536]{2,1,0:T(2,128)(2,1)}), bf16[128,2,1536]{2,1,0:T(2,128)(2,1)S(1)}, u32[]{:S(2)}, u32[]{:S(2)}) async-start(bf16[128,2,1536]{2,1,0:T(2,128)(2,1)} %expert_rows.1), calls=%async_computation.1 | async-start | bytes 1572864 | tf_op jit(solution)/shard_map/all_to_all | solution.py:503

commit v2 on v1

--- a/solution.py
+++ b/solution.py
@@ -89,47 +89,29 @@
 STRIDE = TILE + TILE // 2
 
 
-def payload_kernel(place_ref, *refs):
-    widths = (PATH_COLS, QLORA, HCOLS, HCOLS, LATENT, QLORA)
+def leave_kernel(place_ref, ids_ref, x_ref, nope_ref, comp_ref, rise_q_ref, rise_k_ref, down_k_ref,
+                 down_q_ref, o_ref, same_ref, cross_ref, packed_ref, sent, queued):
+    rep, core = place_ref[0], place_ref[1]
+    gathered = []
     for path in range(2):
-        at = 0
-        for k, width in enumerate(widths):
-            refs[12 + path][:, at : at + width] = refs[6 * path + k][...]
-            at += width
-
-
-def payloads(place, nope, comp, rise_q, rise_k, down_k, down_q):
-    specs = []
-    for path in range(2):
-        quarter = lambda column, path=path: lambda _, p: (p[1] * 2 + path, column)
-        specs += [
-            pl.BlockSpec((ROWS, PATH_COLS), lambda _, p, path=path: (0, (1 - p[0]) * 2 + path)),
-            pl.BlockSpec((ROWS, QLORA), lambda _, p: (0, 0)),
-            pl.BlockSpec((QUARTER, HCOLS), quarter(1)),
-            pl.BlockSpec((QUARTER, HCOLS), quarter(1)),
-            pl.BlockSpec((QUARTER, LATENT), quarter(0)),
-            pl.BlockSpec((QUARTER, QLORA), quarter(0)),
-        ]
-    given = tuple(map(in_hbm, (nope, comp, rise_q, rise_k, down_k, down_q)))
-    return pl.pallas_call(
-        payload_kernel,
-        out_shape=(
-            jax.ShapeDtypeStruct((ROWS, PAYLOAD), bf16),
-            jax.ShapeDtypeStruct((ROWS, PAYLOAD), bf16),
-        ),
-        grid_spec=pltpu.PrefetchScalarGridSpec(
-            num_scalar_prefetch=1,
-            grid=(1,),
-            in_specs=specs,
-            out_specs=(pl.BlockSpec((ROWS, PAYLOAD), lambda _, p: (0, 0)),) * 2,
-        ),
-        compiler_params=params(16),
-        cost_estimate=cost(1 << 10, 1 << 20),
-        name="payloads",
-    )(place, *given, *given)
-
-
-def pack_kernel(ids_ref, x_ref, o_ref, packed_ref, sent):
+        at = pl.multiple_of((1 - rep) * HCOLS + path * PATH_COLS, 128)
+        rows = pl.ds(pl.multiple_of((core * 2 + path) * QUARTER, QUARTER), QUARTER)
+        for source, to, width in (
+            (nope_ref.at[:, pl.ds(at, PATH_COLS)], 0, PATH_COLS),
+            (comp_ref, COMP_AT, QLORA),
+            (rise_q_ref.at[rows, pl.ds(HCOLS, HCOLS)], RISE_Q_AT, HCOLS),
+            (rise_k_ref.at[rows, pl.ds(HCOLS, HCOLS)], RISE_K_AT, HCOLS),
+            (down_k_ref.at[rows, :], DOWN_K_AT, LATENT),
+            (down_q_ref.at[rows, :], DOWN_Q_AT, QLORA),
+        ):
+            copy = pltpu.make_async_copy(
+                source,
+                (same_ref, cross_ref)[path].at[:, pl.ds(to, width)],
+                queued.at[len(gathered)],
+            )
+            copy.start()
+            gathered.append(copy)
+
     mask_a, mask_b = slot_masks(ids_ref[...])
     mask_a, mask_b = mask_a.astype(bf16), mask_b.astype(bf16)
     copies = []
@@ -146,27 +128,36 @@
         )
         copy.start()
         copies.append(copy)
-    for copy in copies:
+    for copy in gathered + copies:
         copy.wait()
 
 
-def pack(ids, x):
+def leave(place, ids, x, nope, comp, rise_q, rise_k, down_k, down_q):
     shape = (EXPERTS, 2, PIECES * SPAN)
+    hbm = pl.BlockSpec(memory_space=pltpu.HBM)
     return pl.pallas_call(
-        pack_kernel,
-        out_shape=pltpu.HBM(shape, bf16),
-        in_specs=[vmem(), vmem()],
-        out_specs=pl.BlockSpec(memory_space=pltpu.HBM),
-        scratch_shapes=[pltpu.VMEM(shape, bf16), pltpu.SemaphoreType.DMA((PIECES,))],
+        leave_kernel,
+        out_shape=(
+            pltpu.HBM(shape, bf16),
+            pltpu.VMEM((ROWS, PAYLOAD), bf16),
+            pltpu.VMEM((ROWS, PAYLOAD), bf16),
+        ),
+        in_specs=[pl.BlockSpec(memory_space=pltpu.SMEM), vmem(), vmem()] + [hbm] * 6,
+        out_specs=(hbm, vmem(), vmem()),
+        scratch_shapes=[
+            pltpu.VMEM(shape, bf16),
+            pltpu.SemaphoreType.DMA((PIECES,)),
+            pltpu.SemaphoreType.DMA((12,)),
+        ],
         compiler_params=params(16),
         cost_estimate=cost(2 * 384 * ROWS * D, 3 * MIB),
-        name="pack_rows",
-    )(ids, x)
-
-
-def expert_kernel(x_ref, w_ref, o_ref, xs_ref, held_ref, sum_ref, came):
+        name="leave",
+    )(place, in_hbm(ids), in_hbm(x), *map(in_hbm, (nope, comp, rise_q, rise_k, down_k, down_q)))
+
+
+def expert_kernel(x_ref, w_ref, o_ref, xs_ref, held_ref, sum_ref, act_ref, came, left):
     rows, wide = 3 * EXPERTS, 2 * TILE
-    copies = []
+    copies, leaving = [], []
     for g in range(PIECES):
         part = pl.ds(g * PIECE, PIECE)
         copy = pltpu.make_async_copy(w_ref.at[0, part, :], held_ref.at[part, :], came.at[g])
@@ -198,8 +189,14 @@
         gate, up = both
         act = (gate / (1.0 + jnp.exp(-gate)) * up).astype(bf16)
         at = n * STRIDE
-        o_ref[:, :, at : at + TILE] = act[: 2 * EXPERTS].reshape(EXPERTS, 2, TILE)
-        o_ref[:, :, at + TILE : at + STRIDE] = act[2 * EXPERTS :].reshape(EXPERTS, 2, TILE // 2)
+        act_ref[:, :, at : at + TILE] = act[: 2 * EXPERTS].reshape(EXPERTS, 2, TILE)
+        act_ref[:, :, at + TILE : at + STRIDE] = act[2 * EXPERTS :].reshape(EXPERTS, 2, TILE // 2)
+        lanes = pl.ds(at, STRIDE)
+        copy = pltpu.make_async_copy(act_ref.at[:, :, lanes], o_ref.at[:, :, lanes], left.at[n])
+        copy.start()
+        leaving.append(copy)
+    for copy in leaving:
+        copy.wait()
 
 
 def expert(x, w):
@@ -209,12 +206,14 @@
         expert_kernel,
         out_shape=pltpu.HBM((EXPERTS, 2, TILES * STRIDE), bf16),
         in_specs=[vmem(), pl.BlockSpec(memory_space=pltpu.HBM)],
-        out_specs=pl.BlockSpec((EXPERTS, 2, TILES * STRIDE), lambda: (0, 0, 0)),
+        out_specs=pl.BlockSpec(memory_space=pltpu.HBM),
         scratch_shapes=[
             pltpu.VMEM((rows, D), bf16),
             pltpu.VMEM((D, 2 * EH), bf16),
             pltpu.VMEM((rows, 2 * EH), f32),
+            pltpu.VMEM((EXPERTS, 2, TILES * STRIDE), bf16),
             pltpu.SemaphoreType.DMA((PIECES,)),
+            pltpu.SemaphoreType.DMA((TILES,)),
         ],
         compiler_params=params(40),
         cost_estimate=cost(2 * rows * D * 2 * EH, 18 * MIB, rows * EH),
@@ -222,7 +221,7 @@
     )(x, in_hbm(w))
 
 
-def unpack_kernel(ids_ref, weight_ref, back_ref, o_ref):
+def picks_kernel(ids_ref, a_ref, b_ref):
     ids = ids_ref[...]
     mask_a, mask_b = slot_masks(ids)
     slot_a = lax.shift_right_logical(
@@ -231,29 +230,50 @@
     slot_b = lax.broadcasted_iota(jnp.int32, (EXPERTS, ROWS), 0)
     pick_a = [jnp.where(ids[c : c + 1, :] == slot_a, mask_a, 0.0) for c in range(TOPK)]
     pick_b = [jnp.where(ids[c : c + 1, :] == slot_b, mask_b, 0.0) for c in range(TOPK)]
-    pick_a = jnp.concatenate(pick_a, axis=1).astype(bf16)
-    pick_b = jnp.concatenate(pick_b, axis=1).astype(bf16)
+    a_ref[...] = jnp.concatenate(pick_a, axis=1).T.astype(bf16)
+    b_ref[...] = jnp.concatenate(pick_b, axis=1).T.astype(bf16)
+
+
+def picks(ids):
+    entries = TOPK * ROWS
+    return pl.pallas_call(
+        picks_kernel,
+        out_shape=(
+            jax.ShapeDtypeStruct((entries, 2 * EXPERTS), bf16),
+            jax.ShapeDtypeStruct((entries, EXPERTS), bf16),
+        ),
+        in_specs=[vmem()],
+        out_specs=(vmem(), vmem()),
+        compiler_params=params(16),
+        cost_estimate=cost(1 << 10, 1 << 10),
+        name="picks",
+    )(ids)
+
+
+def unpack_kernel(pick_a_ref, pick_b_ref, weight_ref, back_ref, o_ref):
     for n in range(TILES):
         at = n * STRIDE
         slots = back_ref[:, :, at : at + TILE].reshape(2 * EXPERTS, TILE)
         third = back_ref[:, :, at + TILE : at + STRIDE].reshape(EXPERTS, TILE)
-        found = contract(pick_a, slots, ((0,), (0,))) + contract(pick_b, third, ((0,), (0,)))
+        found = contract(pick_a_ref[...], slots, ((1,), (0,))) + contract(
+            pick_b_ref[...], third, ((1,), (0,))
+        )
         for c in range(TOPK):
             to = c * EH + n * TILE
             part = weight_ref[:, c : c + 1] * found[c * ROWS : (c + 1) * ROWS]
             o_ref[:, to : to + TILE] = part.astype(bf16)
 
 
-def unpack(ids, weights, back):
+def unpack(pick_a, pick_b, weights, back):
     return pl.pallas_call(
         unpack_kernel,
         out_shape=jax.ShapeDtypeStruct((ROWS, TOPK * EH), bf16),
-        in_specs=[vmem()] * 3,
+        in_specs=[vmem()] * 4,
         out_specs=vmem(),
         compiler_params=params(16),
         cost_estimate=cost(2 * 384 * EXPERTS * EH, 2 * MIB),
         name="unpack_rows",
-    )(ids, weights, back)
+    )(pick_a, pick_b, weights, back)
 
 
 def query_kernel(rep_ref, nope_ref, comp_ref, from_same_ref, from_cross_ref, other_ref, rise_q_ref,
@@ -482,9 +502,10 @@
     to_core = [(e, e ^ 1) for e in range(ep_size)]
 
     factors = (query_rise[0], key_rise[0], key_down[0], query_down[0].T)
-    same, cross = payloads(jnp.stack([rep, core]), query_nope, query_compressed, *factors)
-    moe_input, same, cross = lax.optimization_barrier((moe_input, same, cross))
-    leaving_rows = pack(expert_ids.T, moe_input)
+    ids = expert_ids.T
+    leaving_rows, same, cross = leave(
+        jnp.stack([rep, core]), ids, moe_input, query_nope, query_compressed, *factors
+    )
     arrived_rows = lax.all_to_all(leaving_rows, AXES, 0, 0, tiled=True)
 
     from_same = lax.ppermute(same, AXES, to_same)
@@ -496,13 +517,17 @@
     )
     same = lax.ppermute(same, AXES, to_same)
     cross = lax.ppermute(cross, AXES, to_cross)
-    arrived_rows, own = lax.optimization_barrier((arrived_rows, own))
+    ids, own = lax.optimization_barrier((ids, own))
+    pick_a, pick_b = picks(ids)
+    arrived_rows, own, pick_a, pick_b = lax.optimization_barrier(
+        (arrived_rows, own, pick_a, pick_b)
+    )
     rope = query_rope.reshape(ROWS, HEADS, ROPE)
     activation = expert(arrived_rows, expert_gate_up)
     activation, same, cross = lax.optimization_barrier((activation, same, cross))
     back = lax.all_to_all(activation, AXES, 0, 0, tiled=True)
     attended = attend(cache_lengths, rep.reshape(1), own, same, cross, rope, kv_cache)
-    expert_hidden = unpack(expert_ids.T, route_weights, back)
+    expert_hidden = unpack(pick_a, pick_b, route_weights, back)
     return (attended, expert_hidden)
 
 

time: 89.6 us -> 90.3 us (level)
  waiting for transfers between devices: 26.6 us -> 24.4 us
  starting transfers between devices: 21.6 us -> 23.6 us
  local copies, waits for them, and re-layouts: 3.44 us -> 4.54 us
    all_to_all x1, waiting for transfers between devices: 22.4 us -> 19.2 us  [on_device(): arrived_rows = lax.all_to_all(leaving_rows, AXES, 0, 0, tiled=True)]
    all_to_all x1, starting transfers between devices: 4.7 us -> 6.67 us  [on_device(): back = lax.all_to_all(activation, AXES, 0, 0, tiled=True)]
    unnamed x15 -> x21, local copies, waits for them, and re-layouts: 1.11 us -> 2.34 us
    ppermute x1, starting transfers between devices: 1.15 us -> 2.35 us  [on_device(): other = lax.ppermute(half, 'ep', to_core)]
    ppermute x1, waiting for transfers between devices: 0.01 us -> 1.02 us  [on_device(): from_same = lax.ppermute(same, AXES, to_same)]
  transfers between devices with their start and end apart: 7 -> 7, of which waited for: 3 -> 4; matrix products, arithmetic and copies ran while one was open for 3% -> 3% of each run, Pallas kernels for 36% -> 34%
where the time goes in v2:
time: 90.3 us; the launch traced here: 89.7 us
  Pallas kernels  36.3 us (40%)
  waiting for transfers between devices  24.4 us (27%)
  starting transfers between devices  23.6 us (26%)
  local copies, waits for them, and re-layouts  4.54 us (5%)
    all_to_all x1, waiting for transfers between devices, on_device(): arrived_rows = lax.all_to_all(leaving_rows, AXES, 0, 0, tiled=True)  19.2 us
    pallas_call x1, Pallas kernels, attend(): pl.pallas_call(attend_kernel, out_shape=jax.ShapeDtypeStruct((ROWS, HEADS...  12.8 us
    all_to_all x1, starting transfers between devices, on_device(): arrived_rows = lax.all_to_all(leaving_rows, AXES, 0, 0, tiled=True)  9.95 us
    pallas_call x1, Pallas kernels, expert(): pl.pallas_call(expert_kernel, out_shape=pltpu.HBM((EXPERTS, 2, TILES * ST...  9.44 us
    pallas_call x1, Pallas kernels, query_part(): pl.pallas_call(query_kernel, out_shape=(jax.ShapeDtypeStruct((HALF, ROWS,...  7.47 us
    all_to_all x1, starting transfers between devices, on_device(): back = lax.all_to_all(activation, AXES, 0, 0, tiled=True)  6.67 us
    pallas_call x1, Pallas kernels, leave(): pl.pallas_call(leave_kernel, out_shape=(pltpu.HBM(shape, bf16), pltpu.VME...  4.75 us
    ppermute x1, starting transfers between devices, on_device(): from_cross = lax.ppermute(cross, AXES, to_cross)  3.39 us
  transfers between devices with their start and end apart: 7, of which 4 were waited for; matrix products, arithmetic and copies ran while one was open for 3% of the time, Pallas kernels for 34%

profile of v2, /device:TPU:1, one launch (start us, length us, event | category | flops | bytes accessed | tf_op | source)
XLA Modules:
  0.0 89.7 jit_solution(16391463899441760603)
XLA Ops:
  0.6 0.1 pad_add_fusion.place_ref
  0.7 4.8 %leave.1 = (bf16[128,2,5376]{2,1,0:T(2,128)(2,1)}, bf16[16,13824]{1,0:T(8,128)(2,1)}, bf16[16,13824]{1,0:T(8,128)(2,1)}) custom-call(s32[2]{0:T(128)S(1)} %pad_add_fusion.place_ref, s32[8,16]{1,0:T(8,128)} %bitcast.9, bf16[16,3584]{1,0:T(8,128)(2,1)} %x_ref.1, bf16[16,8192]{1,0:T(8,128)(2,1)} %nope_ref.3, bf16[16,1536]{1,0:T(8,128)(2,1)} %comp_ref.3, ...), custom_call_target="tpu_custom_call" | custom-call | flops 44040192 | bytes 3145728 | tf_op jit(solution)/shard_map/leave/pallas_call | solution.py:138
  5.5 3.4 %collective-permute-start.1 = (bf16[16,13824]{1,0:T(8,128)(2,1)}, bf16[16,13824]{1,0:T(8,128)(2,1)S(1)}, u32[]{:S(2)}, u32[]{:S(2)}) collective-permute-start(bf16[16,13824]{1,0:T(8,128)(2,1)} %get-tuple-element.21), channel_id=1, source_target_pairs={{0,66},{1,67},{2,64},{3,65},{4,70},{5,71},{6,68},{7,69},{8,74},{9,... | collective-permute-start | bytes 1327112 | tf_op jit(solution)/shard_map/ppermute | solution.py:512
  8.9 0.0 collective-permute-start
  8.9 9.9 %all-to-all-start = ((bf16[128,2,5376]{2,1,0:T(2,128)(2,1)}), bf16[128,2,5376]{2,1,0:T(2,128)(2,1)S(1)}, u32[]{:S(2)}, u32[]{:S(2)}) async-start(bf16[128,2,5376]{2,1,0:T(2,128)(2,1)} %get-tuple-element.19), calls=%async_computation | async-start | bytes 5505024 | tf_op jit(solution)/shard_map/all_to_all | solution.py:509
  18.8 0.0 collective-permute-done.1.from_cross_ref
  18.8 0.0 copy-start
  18.9 1.0 %collective-permute-done.from_same_ref = bf16[16,13824]{1,0:T(8,128)(2,1)} collective-permute-done((bf16[16,13824]{1,0:T(8,128)(2,1)}, bf16[16,13824]{1,0:T(8,128)(2,1)}, u32[]{:S(2)}, u32[]{:S(2)}) %collective-permute-start) | collective-permute-done | bytes 442400 | tf_op jit(solution)/shard_map/ppermute | solution.py:511
  19.9 1.0 %slice.8 = bf16[16,10240]{1,0:T(8,128)(2,1)S(1)} slice(bf16[16,13824]{1,0:T(8,128)(2,1)} %collective-permute-done.from_same_ref), slice={[0:16], [3584:13824]} | slice | bytes 655360 | tf_op jit(solution)/shard_map/slice | solution.py:513
  20.9 0.0 copy-start.7
  21.0 2.4 %collective-permute-start.2 = (bf16[32,10240]{1,0:T(8,128)(2,1)S(1)}, bf16[32,10240]{1,0:T(8,128)(2,1)S(1)}, u32[]{:S(2)}, u32[]{:S(2)}) collective-permute-start(bf16[32,10240]{1,0:T(8,128)(2,1)S(1)} %pad_maximum_fusion), channel_id=1, source_target_pairs={{0,1},{1,0},{2,3},{3,2},{4,5},{5,4},{6,7},{7,6},{8,9},{9,8},{10,11... | collective-permute-start | bytes 1966088 | tf_op jit(solution)/shard_map/ppermute | solution.py:514
  23.3 0.0 copy-done
  23.3 1.7 %collective-permute-done.2.other_ref = bf16[32,10240]{1,0:T(8,128)(2,1)S(1)} collective-permute-done((bf16[32,10240]{1,0:T(8,128)(2,1)S(1)}, bf16[32,10240]{1,0:T(8,128)(2,1)S(1)}, u32[]{:S(2)}, u32[]{:S(2)}) %collective-permute-start.2) | collective-permute-done | bytes 655392 | tf_op jit(solution)/shard_map/ppermute | solution.py:514
  25.0 0.0 copy-done.4
  25.0 1.0 %copy-done.1 = bf16[16,13824]{1,0:T(8,128)(2,1)S(1)} copy-done((bf16[16,13824]{1,0:T(8,128)(2,1)S(1)}, bf16[16,13824]{1,0:T(8,128)(2,1)}, u32[]{:S(2)}) %copy-start.1) | copy-done | bytes 442392
  26.1 7.5 %query_latent.1 = (bf16[32,16,512]{2,1,0:T(8,128)(2,1)S(1)}, bf16[16,16,512]{2,1,0:T(8,128)(2,1)}, bf16[16,16,512]{2,1,0:T(8,128)(2,1)}) custom-call(s32[1]{0:T(128)} %bitcast.rep_ref, bf16[16,8192]{1,0:T(8,128)(2,1)} %nope_ref.3, bf16[16,1536]{1,0:T(8,128)(2,1)S(1)} %copy-done.4, bf16[16,13824]{1,0:T(8,128)(2,1)} %collective-permute-done.from_same_ref, ...), custom_call_target="tpu_custom_call" | custom-call | flops 20000000000 | bytes 1024 | tf_op jit(solution)/shard_map/query_latent/pallas_call | solution.py:355
  33.5 0.6 picks.1
  34.1 0.6 copy-done.2
  34.7 0.6 copy-done.5
  35.3 0.0 collective-permute-start.3
  35.4 1.2 %collective-permute-start.4 = (bf16[16,16,512]{2,1,0:T(8,128)(2,1)}, bf16[16,16,512]{2,1,0:T(8,128)(2,1)}, u32[]{:S(2)}, u32[]{:S(2)}) collective-permute-start(bf16[16,16,512]{2,1,0:T(8,128)(2,1)} %get-tuple-element.30), channel_id=1, source_target_pairs={{0,66},{1,67},{2,64},{3,65},{4,70},{5,71},{6,68},{7,69},{8,74},{9,... | collective-permute-start | bytes 786440 | tf_op jit(solution)/shard_map/ppermute | solution.py:519
  36.5 19.2 %all-to-all-done.x_ref = bf16[128,2,5376]{2,1,0:T(2,128)(2,1)S(1)} async-done(((bf16[128,2,5376]{2,1,0:T(2,128)(2,1)}), bf16[128,2,5376]{2,1,0:T(2,128)(2,1)S(1)}, u32[]{:S(2)}, u32[]{:S(2)}) %all-to-all-start) | async-done | bytes 2752544 | tf_op jit(solution)/shard_map/all_to_all | solution.py:509
  55.7 9.4 %expert_rows.1 = bf16[128,2,1536]{2,1,0:T(2,128)(2,1)} custom-call(bf16[128,2,5376]{2,1,0:T(2,128)(2,1)S(1)} %all-to-all-done.x_ref, bf16[1,3584,2048]{2,1,0:T(8,128)(2,1)} %w_ref.1), custom_call_target="tpu_custom_call" | custom-call | flops 5637144576 | bytes 18874368 | tf_op jit(solution)/shard_map/expert_rows/pallas_call | solution.py:205
  65.2 0.0 collective-permute-done.3.same_ref
  65.2 0.0 collective-permute-done.4.cross_ref
  65.2 6.7 %all-to-all-start.1 = ((bf16[128,2,1536]{2,1,0:T(2,128)(2,1)}), bf16[128,2,1536]{2,1,0:T(2,128)(2,1)S(1)}, u32[]{:S(2)}, u32[]{:S(2)}) async-start(bf16[128,2,1536]{2,1,0:T(2,128)(2,1)} %expert_rows.1), calls=%async_computation.1 | async-start | bytes 1572864 | tf_op jit(solution)/shard_map/all_to_all | solution.py:528
  71.9 1.2 %reshape.12.rope_ref = bf16[16,64,64]{2,1,0:T(8,128)(2,1)S(1)} reshape(bf16[16,4096]{1,0:T(8,128)(2,1)} %param.15) | data formatting | bytes 262144 | tf_op jit(solution)/shard_map/reshape | solution.py:525
  73.1 0.0 copy-done.9
  73.1 0.1 copy.16.weight_ref
  73.2 12.8 %attend_rows.1 = bf16[16,32768]{1,0:T(8,128)(2,1)} custom-call(s32[16]{0:T(128)S(1)} %copy-done.8, s32[1]{0:T(128)} %bitcast.rep_ref, bf16[32,16,512]{2,1,0:T(8,128)(2,1)S(1)} %get-tuple-element.27.own_ref, bf16[16,16,512]{2,1,0:T(8,128)(2,1)S(1)} %collective-permute-done.3.same_ref, bf16[16,16,512]{2,1,0:T(8,128)(2,1)} %collective-permute-done.4.cross_ref, ...), custom_call_target="tpu_custom_call" | custom-call | flops 427819008 | bytes 6291456 | tf_op jit(solution)/shard_map/attend_rows/pallas_call | solution.py:454
  85.9 2.5 %all-to-all-done.1.back_ref = bf16[128,2,1536]{2,1,0:T(2,128)(2,1)S(1)} async-done(((bf16[128,2,1536]{2,1,0:T(2,128)(2,1)}), bf16[128,2,1536]{2,1,0:T(2,128)(2,1)S(1)}, u32[]{:S(2)}, u32[]{:S(2)}) %all-to-all-start.1) | async-done | bytes 786464 | tf_op jit(solution)/shard_map/all_to_all | solution.py:528
  88.4 1.3 %unpack_rows.1 = bf16[16,8192]{1,0:T(8,128)(2,1)} custom-call(bf16[128,256]{1,0:T(8,128)(2,1)S(1)} %copy-done.3, bf16[128,128]{1,0:T(8,128)(2,1)S(1)} %copy-done.6, f32[16,8]{1,0:T(8,128)S(1)} %copy.16.weight_ref, bf16[128,2,1536]{2,1,0:T(2,128)(2,1)S(1)} %all-to-all-done.1.back_ref), custom_call_target="tpu_custom_call" | custom-call | flops 100663296 | bytes 2097152 | tf_op jit(solution)/shard_map/unpack_rows/pallas_call | solution.py:268
  (14 shorter events, 0.1 us)
Async XLA Ops:
  5.5 13.4 %collective-permute-start.1 = (bf16[16,13824]{1,0:T(8,128)(2,1)}, bf16[16,13824]{1,0:T(8,128)(2,1)S(1)}, u32[]{:S(2)}, u32[]{:S(2)}) collective-permute-start(bf16[16,13824]{1,0:T(8,128)(2,1)} %get-tuple-element.21), channel_id=1, source_target_pairs={{0,66},{1,67},{2,64},{3,65},{4,70},{5,71},{6,68},{7,69},{8,74},{9,... | collective-permute-start | bytes 1327112 | tf_op jit(solution)/shard_map/ppermute | solution.py:512
  8.9 11.0 %collective-permute-start = (bf16[16,13824]{1,0:T(8,128)(2,1)}, bf16[16,13824]{1,0:T(8,128)(2,1)}, u32[]{:S(2)}, u32[]{:S(2)}) collective-permute-start(bf16[16,13824]{1,0:T(8,128)(2,1)} %get-tuple-element.20), channel_id=1, source_target_pairs={{0,64},{1,65},{2,66},{3,67},{4,68},{5,69},{6,70},{7,71},{8,72},{9,... | collective-permute-start | bytes 1327112 | tf_op jit(solution)/shard_map/ppermute | solution.py:511
  8.9 16.2 %copy-start.4 = (bf16[16,1536]{1,0:T(8,128)(2,1)S(1)}, bf16[16,1536]{1,0:T(8,128)(2,1)}, u32[]{:S(2)}) copy-start(bf16[16,1536]{1,0:T(8,128)(2,1)} %comp_ref.3) | copy-start | bytes 147460
  8.9 46.9 %all-to-all-start = ((bf16[128,2,5376]{2,1,0:T(2,128)(2,1)}), bf16[128,2,5376]{2,1,0:T(2,128)(2,1)S(1)}, u32[]{:S(2)}, u32[]{:S(2)}) async-start(bf16[128,2,5376]{2,1,0:T(2,128)(2,1)} %get-tuple-element.19), calls=%async_computation | async-start | bytes 5505024 | tf_op jit(solution)/shard_map/all_to_all | solution.py:509
  18.8 4.5 %copy-start = (bf16[16,13824]{1,0:T(8,128)(2,1)}, bf16[16,13824]{1,0:T(8,128)(2,1)S(1)}, u32[]{:S(2)}) copy-start(bf16[16,13824]{1,0:T(8,128)(2,1)S(1)} %collective-permute-done.1.from_cross_ref) | copy-start | bytes 1327108
  20.9 12.6 %copy-start.7 = (s32[16,8]{0,1:T(8,128)S(1)}, s32[16,8]{0,1:T(8,128)}, u32[]{:S(2)}) copy-start(s32[16,8]{0,1:T(8,128)} %param.25) | copy-start | bytes 1540
  21.0 4.1 %collective-permute-start.2 = (bf16[32,10240]{1,0:T(8,128)(2,1)S(1)}, bf16[32,10240]{1,0:T(8,128)(2,1)S(1)}, u32[]{:S(2)}, u32[]{:S(2)}) collective-permute-start(bf16[32,10240]{1,0:T(8,128)(2,1)S(1)} %pad_maximum_fusion), channel_id=1, source_target_pairs={{0,1},{1,0},{2,3},{3,2},{4,5},{5,4},{6,7},{7,6},{8,9},{9,8},{10,11... | collective-permute-start | bytes 1966088 | tf_op jit(solution)/shard_map/ppermute | solution.py:514
  25.0 1.0 %copy-start.1 = (bf16[16,13824]{1,0:T(8,128)(2,1)S(1)}, bf16[16,13824]{1,0:T(8,128)(2,1)}, u32[]{:S(2)}) copy-start(bf16[16,13824]{1,0:T(8,128)(2,1)} %copy-done) | copy-start | bytes 1327108
  34.1 0.6 copy-start.2
  34.7 0.6 copy-start.5
  35.3 29.8 %collective-permute-start.3 = (bf16[16,16,512]{2,1,0:T(8,128)(2,1)}, bf16[16,16,512]{2,1,0:T(8,128)(2,1)S(1)}, u32[]{:S(2)}, u32[]{:S(2)}) collective-permute-start(bf16[16,16,512]{2,1,0:T(8,128)(2,1)} %get-tuple-element.29), channel_id=1, source_target_pairs={{0,64},{1,65},{2,66},{3,67},{4,68},{5,69},{6,70},{7,71},{8,72},{9,... | collective-permute-start | bytes 786440 | tf_op jit(solution)/shard_map/ppermute | solution.py:518
  35.4 29.9 %collective-permute-start.4 = (bf16[16,16,512]{2,1,0:T(8,128)(2,1)}, bf16[16,16,512]{2,1,0:T(8,128)(2,1)}, u32[]{:S(2)}, u32[]{:S(2)}) collective-permute-start(bf16[16,16,512]{2,1,0:T(8,128)(2,1)} %get-tuple-element.30), channel_id=1, source_target_pairs={{0,66},{1,67},{2,64},{3,65},{4,70},{5,71},{6,68},{7,69},{8,74},{9,... | collective-permute-start | bytes 786440 | tf_op jit(solution)/shard_map/ppermute | solution.py:519
  55.7 17.3 %copy-start.9 = (f32[16,8]{0,1:T(8,128)S(1)}, f32[16,8]{0,1:T(8,128)}, u32[]{:S(2)}) copy-start(f32[16,8]{0,1:T(8,128)} %param.26) | copy-start | bytes 1540
  55.7 17.4 %copy-start.8 = (s32[16]{0:T(128)S(1)}, s32[16]{0:T(128)}, u32[]{:S(2)}) copy-start(s32[16]{0:T(128)} %lengths_ref.1) | copy-start | bytes 196
  65.2 23.2 %all-to-all-start.1 = ((bf16[128,2,1536]{2,1,0:T(2,128)(2,1)}), bf16[128,2,1536]{2,1,0:T(2,128)(2,1)S(1)}, u32[]{:S(2)}, u32[]{:S(2)}) async-start(bf16[128,2,1536]{2,1,0:T(2,128)(2,1)} %expert_rows.1), calls=%async_computation.1 | async-start | bytes 1572864 | tf_op jit(solution)/shard_map/all_to_all | solution.py:528
  73.2 15.2 %copy-start.3 = (bf16[128,256]{1,0:T(8,128)(2,1)S(1)}, bf16[128,256]{1,0:T(8,128)(2,1)}, u32[]{:S(2)}) copy-start(bf16[128,256]{1,0:T(8,128)(2,1)} %copy-done.2) | copy-start | bytes 196612
  73.2 15.2 %copy-start.6 = (bf16[128,128]{1,0:T(8,128)(2,1)S(1)}, bf16[128,128]{1,0:T(8,128)(2,1)}, u32[]{:S(2)}) copy-start(bf16[128,128]{1,0:T(8,128)(2,1)} %copy-done.5) | copy-start | bytes 98308

commit v3 on v2

--- a/solution.py
+++ b/solution.py
@@ -89,31 +89,57 @@
 STRIDE = TILE + TILE // 2
 
 
-def leave_kernel(place_ref, ids_ref, x_ref, nope_ref, comp_ref, rise_q_ref, rise_k_ref, down_k_ref,
-                 down_q_ref, o_ref, same_ref, cross_ref, packed_ref, sent, queued):
-    rep, core = place_ref[0], place_ref[1]
-    gathered = []
-    for path in range(2):
+def payload_kernel(ids_ref, nope_ref, comp_ref, rise_q_ref, rise_k_ref, down_k_ref, down_q_ref,
+                   same_ref, cross_ref, a_ref, b_ref, held_ref, done):
+    rep, core = lax.axis_index("rep"), lax.rem(lax.axis_index("ep"), 2)
+    named = pltpu.make_async_copy(ids_ref, held_ref, done.at[12])
+    named.start()
+    copies = []
+    for path, target in enumerate((same_ref, cross_ref)):
         at = pl.multiple_of((1 - rep) * HCOLS + path * PATH_COLS, 128)
         rows = pl.ds(pl.multiple_of((core * 2 + path) * QUARTER, QUARTER), QUARTER)
         for source, to, width in (
+            (rise_q_ref.at[rows, pl.ds(HCOLS, HCOLS)], RISE_Q_AT, HCOLS),
+            (rise_k_ref.at[rows, pl.ds(HCOLS, HCOLS)], RISE_K_AT, HCOLS),
             (nope_ref.at[:, pl.ds(at, PATH_COLS)], 0, PATH_COLS),
             (comp_ref, COMP_AT, QLORA),
-            (rise_q_ref.at[rows, pl.ds(HCOLS, HCOLS)], RISE_Q_AT, HCOLS),
-            (rise_k_ref.at[rows, pl.ds(HCOLS, HCOLS)], RISE_K_AT, HCOLS),
             (down_k_ref.at[rows, :], DOWN_K_AT, LATENT),
             (down_q_ref.at[rows, :], DOWN_Q_AT, QLORA),
         ):
             copy = pltpu.make_async_copy(
-                source,
-                (same_ref, cross_ref)[path].at[:, pl.ds(to, width)],
-                queued.at[len(gathered)],
+                source, target.at[:, pl.ds(to, width)], done.at[len(copies)]
             )
             copy.start()
-            gathered.append(copy)
-
-    mask_a, mask_b = slot_masks(ids_ref[...])
-    mask_a, mask_b = mask_a.astype(bf16), mask_b.astype(bf16)
+            copies.append(copy)
+    named.wait()
+    mask_a, mask_b = slot_masks(held_ref[...])
+    a_ref[...] = mask_a.astype(bf16)
+    b_ref[...] = mask_b.astype(bf16)
+    for copy in copies:
+        copy.wait()
+
+
+def payloads(ids, nope, comp, rise_q, rise_k, down_k, down_q):
+    hbm = pl.BlockSpec(memory_space=pltpu.HBM)
+    return pl.pallas_call(
+        payload_kernel,
+        out_shape=(
+            jax.ShapeDtypeStruct((ROWS, PAYLOAD), bf16),
+            jax.ShapeDtypeStruct((ROWS, PAYLOAD), bf16),
+            jax.ShapeDtypeStruct((2 * EXPERTS, ROWS), bf16),
+            jax.ShapeDtypeStruct((EXPERTS, ROWS), bf16),
+        ),
+        in_specs=[hbm] * 7,
+        out_specs=(vmem(),) * 4,
+        scratch_shapes=[pltpu.VMEM((TOPK, ROWS), jnp.int32), pltpu.SemaphoreType.DMA((13,))],
+        compiler_params=params(16),
+        cost_estimate=cost(1 << 10, 1 << 20),
+        name="payloads",
+    )(*map(in_hbm, (ids, nope, comp, rise_q, rise_k, down_k, down_q)))
+
+
+def pack_kernel(a_ref, b_ref, x_ref, o_ref, packed_ref, sent):
+    mask_a, mask_b = a_ref[...], b_ref[...]
     copies = []
     for g in range(PIECES):
         x = x_ref[:, g * PIECE : (g + 1) * PIECE]
@@ -128,31 +154,22 @@
         )
         copy.start()
         copies.append(copy)
-    for copy in gathered + copies:
+    for copy in copies:
         copy.wait()
 
 
-def leave(place, ids, x, nope, comp, rise_q, rise_k, down_k, down_q):
+def pack(mask_a, mask_b, x):
     shape = (EXPERTS, 2, PIECES * SPAN)
-    hbm = pl.BlockSpec(memory_space=pltpu.HBM)
-    return pl.pallas_call(
-        leave_kernel,
-        out_shape=(
-            pltpu.HBM(shape, bf16),
-            pltpu.VMEM((ROWS, PAYLOAD), bf16),
-            pltpu.VMEM((ROWS, PAYLOAD), bf16),
-        ),
-        in_specs=[pl.BlockSpec(memory_space=pltpu.SMEM), vmem(), vmem()] + [hbm] * 6,
-        out_specs=(hbm, vmem(), vmem()),
-        scratch_shapes=[
-            pltpu.VMEM(shape, bf16),
-            pltpu.SemaphoreType.DMA((PIECES,)),
-            pltpu.SemaphoreType.DMA((12,)),
-        ],
+    return pl.pallas_call(
+        pack_kernel,
+        out_shape=pltpu.HBM(shape, bf16),
+        in_specs=[vmem(), vmem(), vmem()],
+        out_specs=pl.BlockSpec(memory_space=pltpu.HBM),
+        scratch_shapes=[pltpu.VMEM(shape, bf16), pltpu.SemaphoreType.DMA((PIECES,))],
         compiler_params=params(16),
         cost_estimate=cost(2 * 384 * ROWS * D, 3 * MIB),
-        name="leave",
-    )(place, in_hbm(ids), in_hbm(x), *map(in_hbm, (nope, comp, rise_q, rise_k, down_k, down_q)))
+        name="pack_rows",
+    )(mask_a, mask_b, x)
 
 
 def expert_kernel(x_ref, w_ref, o_ref, xs_ref, held_ref, sum_ref, act_ref, came, left):
@@ -473,7 +490,7 @@
         compiler_params=params(40),
         cost_estimate=cost(2 * ROWS * HEADS * LEN * 1088, 6 * MIB, ROWS * HEADS * LEN),
         name="attend_rows",
-    )(lengths, rep, own, same, cross, rope, in_hbm(kv))
+    )(lengths, rep, own, in_hbm(same), in_hbm(cross), rope, in_hbm(kv))
 
 
 def on_device(
@@ -493,7 +510,6 @@
     expert_gate_up,
 ):
     rep = lax.axis_index("rep")
-    core = lax.axis_index("ep") % 2
     ep_size = lax.axis_size("ep")
     every = [(r, e) for r in range(2) for e in range(ep_size)]
     place = lambda r, e: r * ep_size + e
@@ -503,9 +519,9 @@
 
     factors = (query_rise[0], key_rise[0], key_down[0], query_down[0].T)
     ids = expert_ids.T
-    leaving_rows, same, cross = leave(
-        jnp.stack([rep, core]), ids, moe_input, query_nope, query_compressed, *factors
-    )
+    same, cross, mask_a, mask_b = payloads(ids, query_nope, query_compressed, *factors)
+    moe_input, same, cross = lax.optimization_barrier((moe_input, same, cross))
+    leaving_rows = pack(mask_a, mask_b, moe_input)
     arrived_rows = lax.all_to_all(leaving_rows, AXES, 0, 0, tiled=True)
 
     from_same = lax.ppermute(same, AXES, to_same)

time: 90.3 us -> 88.4 us (0.979)
  local copies, waits for them, and re-layouts: 4.54 us -> 2.5 us
  starting transfers between devices: 23.6 us -> 21.7 us
  waiting for transfers between devices: 24.4 us -> 25.8 us
    all_to_all x1, starting transfers between devices: 6.67 us -> 4.7 us  [on_device(): back = lax.all_to_all(activation, AXES, 0, 0, tiled=True)]
    ppermute x1, starting transfers between devices: 2.35 us -> 1.07 us  [on_device(): other = lax.ppermute(half, 'ep', to_core)]
    all_to_all x1, waiting for transfers between devices: 19.2 us -> 20.4 us  [on_device(): arrived_rows = lax.all_to_all(leaving_rows, AXES, 0, 0, tiled=True)]
    unnamed x21 -> x17, local copies, waits for them, and re-layouts: 2.34 us -> 1.12 us
    ppermute x1, waiting for transfers between devices: 1.02 us -> 0.01 us  [on_device(): from_same = lax.ppermute(same, AXES, to_same)]
    reshape x1, local copies, waits for them, and re-layouts: 1.18 us -> 0.24 us  [on_device(): rope = query_rope.reshape(ROWS, HEADS, ROPE)]
    pallas_call x1 -> x2, Pallas kernels: 4.75 us -> 4.38 us  [the longest x1 2.27 us: payloads(): pl.pallas_call(payload_kernel, out_shape=(jax.ShapeDtypeStruct((ROWS, PAY...]
  transfers between devices with their start and end apart: 7 -> 7, of which waited for: 4 -> 3; matrix products, arithmetic and copies ran while one was open for 3% -> 3% of each run, Pallas kernels for 34% -> 37%
where the time goes in v3:
time: 88.4 us; the launch traced here: 87.9 us
  Pallas kernels  36.3 us (41%)
  waiting for transfers between devices  25.8 us (29%)
  starting transfers between devices  21.7 us (25%)
  local copies, waits for them, and re-layouts  2.5 us (3%)
    all_to_all x1, waiting for transfers between devices, on_device(): arrived_rows = lax.all_to_all(leaving_rows, AXES, 0, 0, tiled=True)  20.4 us
    pallas_call x1, Pallas kernels, attend(): pl.pallas_call(attend_kernel, out_shape=jax.ShapeDtypeStruct((ROWS, HEADS...  12.9 us
    all_to_all x1, starting transfers between devices, on_device(): arrived_rows = lax.all_to_all(leaving_rows, AXES, 0, 0, tiled=True)  9.95 us
    pallas_call x1, Pallas kernels, expert(): pl.pallas_call(expert_kernel, out_shape=pltpu.HBM((EXPERTS, 2, TILES * ST...  9.46 us
    pallas_call x1, Pallas kernels, query_part(): pl.pallas_call(query_kernel, out_shape=(jax.ShapeDtypeStruct((HALF, ROWS,...  7.71 us
    all_to_all x1, starting transfers between devices, on_device(): back = lax.all_to_all(activation, AXES, 0, 0, tiled=True)  4.7 us
    ppermute x1, starting transfers between devices, on_device(): from_cross = lax.ppermute(cross, AXES, to_cross)  3.39 us
    all_to_all x1, waiting for transfers between devices, on_device(): back = lax.all_to_all(activation, AXES, 0, 0, tiled=True)  3.31 us
  transfers between devices with their start and end apart: 7, of which 3 were waited for; matrix products, arithmetic and copies ran while one was open for 3% of the time, Pallas kernels for 37%

profile of v3, /device:TPU:1, one launch (start us, length us, event | category | flops | bytes accessed | tf_op | source)
XLA Modules:
  0.0 87.9 jit_solution(17209282973107395072)
XLA Ops:
  0.6 0.0 copy-start.2
  0.6 2.3 %payloads.1 = (bf16[16,13824]{1,0:T(8,128)(2,1)}, bf16[16,13824]{1,0:T(8,128)(2,1)}, bf16[256,16]{1,0:T(8,128)(2,1)S(1)}, bf16[128,16]{1,0:T(8,128)(2,1)S(1)}) custom-call(s32[8,16]{1,0:T(8,128)} %bitcast.8, bf16[16,8192]{1,0:T(8,128)(2,1)} %nope_ref.3, bf16[16,1536]{1,0:T(8,128)(2,1)} %comp_ref.3, bf16[64,8192]{1,0:T(8,128)(2,1)} %bitcast.10, ...), custom_call_target="tpu_custom_call" | custom-call | flops 1024 | bytes 1048576 | tf_op jit(solution)/shard_map/payloads/pallas_call | solution.py:124
  2.9 3.4 %collective-permute-start.1 = (bf16[16,13824]{1,0:T(8,128)(2,1)}, bf16[16,13824]{1,0:T(8,128)(2,1)S(1)}, u32[]{:S(2)}, u32[]{:S(2)}) collective-permute-start(bf16[16,13824]{1,0:T(8,128)(2,1)} %get-tuple-element.29), channel_id=1, source_target_pairs={{0,66},{1,67},{2,64},{3,65},{4,70},{5,71},{6,68},{7,69},{8,74},{9,... | collective-permute-start | bytes 1327112 | tf_op jit(solution)/shard_map/ppermute | solution.py:528
  6.3 0.0 collective-permute-start
  6.3 0.0 copy-done.2
  6.3 2.1 %pack_rows.1 = bf16[128,2,5376]{2,1,0:T(2,128)(2,1)} custom-call(bf16[256,16]{1,0:T(8,128)(2,1)S(1)} %get-tuple-element.23.a_ref, bf16[128,16]{1,0:T(8,128)(2,1)S(1)} %get-tuple-element.24.b_ref, bf16[16,3584]{1,0:T(8,128)(2,1)S(1)} %copy-done.2), custom_call_target="tpu_custom_call" | custom-call | flops 44040192 | bytes 3145728 | tf_op jit(solution)/shard_map/pack_rows/pallas_call | solution.py:163
  8.4 0.0 copy-start.3
  8.4 10.0 %all-to-all-start = ((bf16[128,2,5376]{2,1,0:T(2,128)(2,1)}), bf16[128,2,5376]{2,1,0:T(2,128)(2,1)S(1)}, u32[]{:S(2)}, u32[]{:S(2)}) async-start(bf16[128,2,5376]{2,1,0:T(2,128)(2,1)} %pack_rows.1), calls=%async_computation | async-start | bytes 5505024 | tf_op jit(solution)/shard_map/all_to_all | solution.py:525
  18.4 0.0 collective-permute-done.1.from_cross_ref
  18.4 0.0 copy-start
  18.5 0.0 collective-permute-done.from_same_ref
  18.5 1.1 %slice.8 = bf16[16,10240]{1,0:T(8,128)(2,1)S(1)} slice(bf16[16,13824]{1,0:T(8,128)(2,1)} %collective-permute-done.from_same_ref), slice={[0:16], [3584:13824]} | slice | bytes 655360 | tf_op jit(solution)/shard_map/slice | solution.py:529
  19.6 0.9 %pad_maximum_fusion = bf16[32,10240]{1,0:T(8,128)(2,1)} fusion(bf16[16,10240]{1,0:T(8,128)(2,1)S(1)} %slice.9, bf16[16,10240]{1,0:T(8,128)(2,1)S(1)} %slice.8), kind=kLoop, calls=%fused_computation | loop fusion | flops 1310720 | bytes 1310720 | tf_op jit(solution)/shard_map/concatenate | solution.py:529
  20.5 1.1 %collective-permute-start.2 = (bf16[32,10240]{1,0:T(8,128)(2,1)}, bf16[32,10240]{1,0:T(8,128)(2,1)}, u32[]{:S(2)}, u32[]{:S(2)}) collective-permute-start(bf16[32,10240]{1,0:T(8,128)(2,1)} %pad_maximum_fusion), channel_id=1, source_target_pairs={{0,1},{1,0},{2,3},{3,2},{4,5},{5,4},{6,7},{7,6},{8,9},{9,8},{10,11... | collective-permute-start | bytes 1966088 | tf_op jit(solution)/shard_map/ppermute | solution.py:530
  21.5 2.1 %collective-permute-done.2.other_ref = bf16[32,10240]{1,0:T(8,128)(2,1)} collective-permute-done((bf16[32,10240]{1,0:T(8,128)(2,1)}, bf16[32,10240]{1,0:T(8,128)(2,1)}, u32[]{:S(2)}, u32[]{:S(2)}) %collective-permute-start.2) | collective-permute-done | bytes 655392 | tf_op jit(solution)/shard_map/ppermute | solution.py:530
  23.6 0.0 copy-done
  23.6 1.0 %copy-done.1 = bf16[16,13824]{1,0:T(8,128)(2,1)S(1)} copy-done((bf16[16,13824]{1,0:T(8,128)(2,1)S(1)}, bf16[16,13824]{1,0:T(8,128)(2,1)}, u32[]{:S(2)}) %copy-start.1) | copy-done | bytes 442392
  24.6 7.7 %query_latent.1 = (bf16[32,16,512]{2,1,0:T(8,128)(2,1)S(1)}, bf16[16,16,512]{2,1,0:T(8,128)(2,1)}, bf16[16,16,512]{2,1,0:T(8,128)(2,1)}) custom-call(s32[1]{0:T(128)} %bitcast.rep_ref, bf16[16,8192]{1,0:T(8,128)(2,1)} %nope_ref.3, bf16[16,1536]{1,0:T(8,128)(2,1)S(1)} %copy-done.3, bf16[16,13824]{1,0:T(8,128)(2,1)} %collective-permute-done.from_same_ref, ...), custom_call_target="tpu_custom_call" | custom-call | flops 20000000000 | bytes 1024 | tf_op jit(solution)/shard_map/query_latent/pallas_call | solution.py:372
  32.3 0.6 picks.1
  32.9 0.8 collective-permute-start.3
  33.7 1.8 %collective-permute-start.4 = (bf16[16,16,512]{2,1,0:T(8,128)(2,1)}, bf16[16,16,512]{2,1,0:T(8,128)(2,1)}, u32[]{:S(2)}, u32[]{:S(2)}) collective-permute-start(bf16[16,16,512]{2,1,0:T(8,128)(2,1)} %get-tuple-element.38), channel_id=1, source_target_pairs={{0,66},{1,67},{2,64},{3,65},{4,70},{5,71},{6,68},{7,69},{8,74},{9,... | collective-permute-start | bytes 786440 | tf_op jit(solution)/shard_map/ppermute | solution.py:535
  35.5 20.4 %all-to-all-done.x_ref = bf16[128,2,5376]{2,1,0:T(2,128)(2,1)S(1)} async-done(((bf16[128,2,5376]{2,1,0:T(2,128)(2,1)}), bf16[128,2,5376]{2,1,0:T(2,128)(2,1)S(1)}, u32[]{:S(2)}, u32[]{:S(2)}) %all-to-all-start) | async-done | bytes 2752544 | tf_op jit(solution)/shard_map/all_to_all | solution.py:525
  55.9 9.5 %expert_rows.1 = bf16[128,2,1536]{2,1,0:T(2,128)(2,1)} custom-call(bf16[128,2,5376]{2,1,0:T(2,128)(2,1)S(1)} %all-to-all-done.x_ref, bf16[1,3584,2048]{2,1,0:T(8,128)(2,1)} %w_ref.1), custom_call_target="tpu_custom_call" | custom-call | flops 5637144576 | bytes 18874368 | tf_op jit(solution)/shard_map/expert_rows/pallas_call | solution.py:222
  65.4 0.0 collective-permute-done.3.same_ref
  65.4 0.0 collective-permute-done.4.cross_ref
  65.4 4.7 %all-to-all-start.1 = ((bf16[128,2,1536]{2,1,0:T(2,128)(2,1)}), bf16[128,2,1536]{2,1,0:T(2,128)(2,1)S(1)}, u32[]{:S(2)}, u32[]{:S(2)}) async-start(bf16[128,2,1536]{2,1,0:T(2,128)(2,1)} %expert_rows.1), calls=%async_computation.1 | async-start | bytes 1572864 | tf_op jit(solution)/shard_map/all_to_all | solution.py:544
  70.1 0.2 reshape.12.rope_ref
  70.4 0.1 copy.16.weight_ref
  70.4 0.0 copy-done.5
  70.4 12.9 %attend_rows.1 = bf16[16,32768]{1,0:T(8,128)(2,1)} custom-call(s32[16]{0:T(128)S(1)} %copy-done.5, s32[1]{0:T(128)} %bitcast.rep_ref, bf16[32,16,512]{2,1,0:T(8,128)(2,1)S(1)} %get-tuple-element.35.own_ref, bf16[16,16,512]{2,1,0:T(8,128)(2,1)} %collective-permute-done.3.same_ref, bf16[16,16,512]{2,1,0:T(8,128)(2,1)} %collective-permute-done.4.cross_ref, ...), custom_call_target="tpu_custom_call" | custom-call | flops 427819008 | bytes 6291456 | tf_op jit(solution)/shard_map/attend_rows/pallas_call | solution.py:471
  83.3 3.3 %all-to-all-done.1.back_ref = bf16[128,2,1536]{2,1,0:T(2,128)(2,1)S(1)} async-done(((bf16[128,2,1536]{2,1,0:T(2,128)(2,1)}), bf16[128,2,1536]{2,1,0:T(2,128)(2,1)S(1)}, u32[]{:S(2)}, u32[]{:S(2)}) %all-to-all-start.1) | async-done | bytes 786464 | tf_op jit(solution)/shard_map/all_to_all | solution.py:544
  86.6 1.3 %unpack_rows.1 = bf16[16,8192]{1,0:T(8,128)(2,1)} custom-call(bf16[128,256]{1,0:T(8,128)(2,1)S(1)} %get-tuple-element.41.pick_a_ref, bf16[128,128]{1,0:T(8,128)(2,1)S(1)} %get-tuple-element.42.pick_b_ref, f32[16,8]{1,0:T(8,128)S(1)} %copy.16.weight_ref, bf16[128,2,1536]{2,1,0:T(2,128)(2,1)S(1)} %all-to-all-done.1.back_ref), custom_call_target="tpu_custom_call" | custom-call | flops 100663296 | bytes 2097152 | tf_op jit(solution)/shard_map/unpack_rows/pallas_call | solution.py:285
  (10 shorter events, 0.0 us)
Async XLA Ops:
  0.6 5.7 %copy-start.2 = (bf16[16,3584]{1,0:T(8,128)(2,1)S(1)}, bf16[16,3584]{1,0:T(8,128)(2,1)}, u32[]{:S(2)}) copy-start(bf16[16,3584]{1,0:T(8,128)(2,1)} %x_ref) | copy-start | bytes 344068
  2.9 15.5 %collective-permute-start.1 = (bf16[16,13824]{1,0:T(8,128)(2,1)}, bf16[16,13824]{1,0:T(8,128)(2,1)S(1)}, u32[]{:S(2)}, u32[]{:S(2)}) collective-permute-start(bf16[16,13824]{1,0:T(8,128)(2,1)} %get-tuple-element.29), channel_id=1, source_target_pairs={{0,66},{1,67},{2,64},{3,65},{4,70},{5,71},{6,68},{7,69},{8,74},{9,... | collective-permute-start | bytes 1327112 | tf_op jit(solution)/shard_map/ppermute | solution.py:528
  6.3 12.1 %collective-permute-start = (bf16[16,13824]{1,0:T(8,128)(2,1)}, bf16[16,13824]{1,0:T(8,128)(2,1)}, u32[]{:S(2)}, u32[]{:S(2)}) collective-permute-start(bf16[16,13824]{1,0:T(8,128)(2,1)} %get-tuple-element.28), channel_id=1, source_target_pairs={{0,64},{1,65},{2,66},{3,67},{4,68},{5,69},{6,70},{7,71},{8,72},{9,... | collective-permute-start | bytes 1327112 | tf_op jit(solution)/shard_map/ppermute | solution.py:527
  8.4 15.2 %copy-start.3 = (bf16[16,1536]{1,0:T(8,128)(2,1)S(1)}, bf16[16,1536]{1,0:T(8,128)(2,1)}, u32[]{:S(2)}) copy-start(bf16[16,1536]{1,0:T(8,128)(2,1)} %comp_ref.3) | copy-start | bytes 147460
  8.4 47.5 %all-to-all-start = ((bf16[128,2,5376]{2,1,0:T(2,128)(2,1)}), bf16[128,2,5376]{2,1,0:T(2,128)(2,1)S(1)}, u32[]{:S(2)}, u32[]{:S(2)}) async-start(bf16[128,2,5376]{2,1,0:T(2,128)(2,1)} %pack_rows.1), calls=%async_computation | async-start | bytes 5505024 | tf_op jit(solution)/shard_map/all_to_all | solution.py:525
  18.4 5.2 %copy-start = (bf16[16,13824]{1,0:T(8,128)(2,1)}, bf16[16,13824]{1,0:T(8,128)(2,1)S(1)}, u32[]{:S(2)}) copy-start(bf16[16,13824]{1,0:T(8,128)(2,1)S(1)} %collective-permute-done.1.from_cross_ref) | copy-start | bytes 1327108
  20.5 3.1 %collective-permute-start.2 = (bf16[32,10240]{1,0:T(8,128)(2,1)}, bf16[32,10240]{1,0:T(8,128)(2,1)}, u32[]{:S(2)}, u32[]{:S(2)}) collective-permute-start(bf16[32,10240]{1,0:T(8,128)(2,1)} %pad_maximum_fusion), channel_id=1, source_target_pairs={{0,1},{1,0},{2,3},{3,2},{4,5},{5,4},{6,7},{7,6},{8,9},{9,8},{10,11... | collective-permute-start | bytes 1966088 | tf_op jit(solution)/shard_map/ppermute | solution.py:530
  23.6 1.0 %copy-start.1 = (bf16[16,13824]{1,0:T(8,128)(2,1)S(1)}, bf16[16,13824]{1,0:T(8,128)(2,1)}, u32[]{:S(2)}) copy-start(bf16[16,13824]{1,0:T(8,128)(2,1)} %copy-done) | copy-start | bytes 1327108
  24.6 7.7 %copy-start.4 = (s32[16,8]{0,1:T(8,128)S(1)}, s32[16,8]{0,1:T(8,128)}, u32[]{:S(2)}) copy-start(s32[16,8]{0,1:T(8,128)} %param.25) | copy-start | bytes 1540
  32.9 32.4 %collective-permute-start.3 = (bf16[16,16,512]{2,1,0:T(8,128)(2,1)}, bf16[16,16,512]{2,1,0:T(8,128)(2,1)}, u32[]{:S(2)}, u32[]{:S(2)}) collective-permute-start(bf16[16,16,512]{2,1,0:T(8,128)(2,1)} %get-tuple-element.37), channel_id=1, source_target_pairs={{0,64},{1,65},{2,66},{3,67},{4,68},{5,69},{6,70},{7,71},{8,72},{9,... | collective-permute-start | bytes 786440 | tf_op jit(solution)/shard_map/ppermute | solution.py:534
  33.7 31.7 %collective-permute-start.4 = (bf16[16,16,512]{2,1,0:T(8,128)(2,1)}, bf16[16,16,512]{2,1,0:T(8,128)(2,1)}, u32[]{:S(2)}, u32[]{:S(2)}) collective-permute-start(bf16[16,16,512]{2,1,0:T(8,128)(2,1)} %get-tuple-element.38), channel_id=1, source_target_pairs={{0,66},{1,67},{2,64},{3,65},{4,70},{5,71},{6,68},{7,69},{8,74},{9,... | collective-permute-start | bytes 786440 | tf_op jit(solution)/shard_map/ppermute | solution.py:535
  55.9 14.2 %copy-start.6 = (bf16[16,4096]{1,0:T(8,128)(2,1)S(1)}, bf16[16,4096]{1,0:T(8,128)(2,1)}, u32[]{:S(2)}) copy-start(bf16[16,4096]{1,0:T(8,128)(2,1)} %param.15) | copy-start | bytes 393220
  55.9 14.5 %copy-start.7 = (f32[16,8]{0,1:T(8,128)S(1)}, f32[16,8]{0,1:T(8,128)}, u32[]{:S(2)}) copy-start(f32[16,8]{0,1:T(8,128)} %param.26) | copy-start | bytes 1540
  55.9 14.5 %copy-start.5 = (s32[16]{0:T(128)S(1)}, s32[16]{0:T(128)}, u32[]{:S(2)}) copy-start(s32[16]{0:T(128)} %lengths_ref.1) | copy-start | bytes 196
  65.4 21.2 %all-to-all-start.1 = ((bf16[128,2,1536]{2,1,0:T(2,128)(2,1)}), bf16[128,2,1536]{2,1,0:T(2,128)(2,1)S(1)}, u32[]{:S(2)}, u32[]{:S(2)}) async-start(bf16[128,2,1536]{2,1,0:T(2,128)(2,1)} %expert_rows.1), calls=%async_computation.1 | async-start | bytes 1572864 | tf_op jit(solution)/shard_map/all_to_all | solution.py:544

commit v4 on v3

--- a/solution.py
+++ b/solution.py
@@ -82,7 +82,8 @@
 
 PIECE = 512
 PIECES = D // PIECE
-TAKEN = (1, 1, 2, 2, 1)
+PART = 256
+TAKEN = (1, 2, 3, 4, 4)
 SPAN = PIECE + PIECE // 2
 TILE = 256
 TILES = EH // TILE
@@ -175,8 +176,8 @@
 def expert_kernel(x_ref, w_ref, o_ref, xs_ref, held_ref, sum_ref, act_ref, came, left):
     rows, wide = 3 * EXPERTS, 2 * TILE
     copies, leaving = [], []
-    for g in range(PIECES):
-        part = pl.ds(g * PIECE, PIECE)
+    for g in range(D // PART):
+        part = pl.ds(g * PART, PART)
         copy = pltpu.make_async_copy(w_ref.at[0, part, :], held_ref.at[part, :], came.at[g])
         copy.start()
         copies.append(copy)
@@ -188,15 +189,15 @@
     for take in TAKEN[:-1]:
         for g in range(done, done + take):
             copies[g].wait()
-        part = slice(done * PIECE, (done + take) * PIECE)
+        part = slice(done * PART, (done + take) * PART)
         for n in range(2 * EH // wide):
             to = slice(n * wide, (n + 1) * wide)
             term = contract(xs_ref[:, part], held_ref[part, to], ((1,), (0,)))
             sum_ref[:, to] = term if done == 0 else sum_ref[:, to] + term
         done += take
-    for g in range(done, PIECES):
+    for g in range(done, D // PART):
         copies[g].wait()
-    part = slice(done * PIECE, D)
+    part = slice(done * PART, D)
     for n in range(TILES):
         both = []
         for k in range(2):
@@ -229,7 +230,7 @@
             pltpu.VMEM((D, 2 * EH), bf16),
             pltpu.VMEM((rows, 2 * EH), f32),
             pltpu.VMEM((EXPERTS, 2, TILES * STRIDE), bf16),
-            pltpu.SemaphoreType.DMA((PIECES,)),
+            pltpu.SemaphoreType.DMA((D // PART,)),
             pltpu.SemaphoreType.DMA((TILES,)),
         ],
         compiler_params=params(40),

time: 88.4 us -> 88.2 us (level)
  no operation moved by 1% of the time
where the time goes in v4:
time: 88.2 us; the launch traced here: 87.6 us
  Pallas kernels  36 us (41%)
  waiting for transfers between devices  25.8 us (29%)
  starting transfers between devices  21.7 us (25%)
  local copies, waits for them, and re-layouts  2.5 us (3%)
    all_to_all x1, waiting for transfers between devices, on_device(): arrived_rows = lax.all_to_all(leaving_rows, AXES, 0, 0, tiled=True)  20.4 us
    pallas_call x1, Pallas kernels, attend(): pl.pallas_call(attend_kernel, out_shape=jax.ShapeDtypeStruct((ROWS, HEADS...  12.9 us
    all_to_all x1, starting transfers between devices, on_device(): arrived_rows = lax.all_to_all(leaving_rows, AXES, 0, 0, tiled=True)  9.95 us
    pallas_call x1, Pallas kernels, expert(): pl.pallas_call(expert_kernel, out_shape=pltpu.HBM((EXPERTS, 2, TILES * ST...  9.2 us
    pallas_call x1, Pallas kernels, query_part(): pl.pallas_call(query_kernel, out_shape=(jax.ShapeDtypeStruct((HALF, ROWS,...  7.71 us
    all_to_all x1, starting transfers between devices, on_device(): back = lax.all_to_all(activation, AXES, 0, 0, tiled=True)  4.7 us
    ppermute x1, starting transfers between devices, on_device(): from_cross = lax.ppermute(cross, AXES, to_cross)  3.39 us
    all_to_all x1, waiting for transfers between devices, on_device(): back = lax.all_to_all(activation, AXES, 0, 0, tiled=True)  3.31 us
  transfers between devices with their start and end apart: 7, of which 3 were waited for; matrix products, arithmetic and copies ran while one was open for 3% of the time, Pallas kernels for 37%

profile of v4, /device:TPU:1, one launch (start us, length us, event | category | flops | bytes accessed | tf_op | source)
XLA Modules:
  0.0 87.6 jit_solution(7673505350487610650)
XLA Ops:
  0.6 0.0 copy-start.2
  0.6 2.3 %payloads.1 = (bf16[16,13824]{1,0:T(8,128)(2,1)}, bf16[16,13824]{1,0:T(8,128)(2,1)}, bf16[256,16]{1,0:T(8,128)(2,1)S(1)}, bf16[128,16]{1,0:T(8,128)(2,1)S(1)}) custom-call(s32[8,16]{1,0:T(8,128)} %bitcast.8, bf16[16,8192]{1,0:T(8,128)(2,1)} %nope_ref.3, bf16[16,1536]{1,0:T(8,128)(2,1)} %comp_ref.3, bf16[64,8192]{1,0:T(8,128)(2,1)} %bitcast.10, ...), custom_call_target="tpu_custom_call" | custom-call | flops 1024 | bytes 1048576 | tf_op jit(solution)/shard_map/payloads/pallas_call | solution.py:125
  2.9 3.4 %collective-permute-start.1 = (bf16[16,13824]{1,0:T(8,128)(2,1)}, bf16[16,13824]{1,0:T(8,128)(2,1)S(1)}, u32[]{:S(2)}, u32[]{:S(2)}) collective-permute-start(bf16[16,13824]{1,0:T(8,128)(2,1)} %get-tuple-element.29), channel_id=1, source_target_pairs={{0,66},{1,67},{2,64},{3,65},{4,70},{5,71},{6,68},{7,69},{8,74},{9,... | collective-permute-start | bytes 1327112 | tf_op jit(solution)/shard_map/ppermute | solution.py:529
  6.3 0.0 collective-permute-start
  6.3 0.0 copy-done.2
  6.3 2.1 %pack_rows.1 = bf16[128,2,5376]{2,1,0:T(2,128)(2,1)} custom-call(bf16[256,16]{1,0:T(8,128)(2,1)S(1)} %get-tuple-element.23.a_ref, bf16[128,16]{1,0:T(8,128)(2,1)S(1)} %get-tuple-element.24.b_ref, bf16[16,3584]{1,0:T(8,128)(2,1)S(1)} %copy-done.2), custom_call_target="tpu_custom_call" | custom-call | flops 44040192 | bytes 3145728 | tf_op jit(solution)/shard_map/pack_rows/pallas_call | solution.py:164
  8.4 0.0 copy-start.3
  8.4 10.0 %all-to-all-start = ((bf16[128,2,5376]{2,1,0:T(2,128)(2,1)}), bf16[128,2,5376]{2,1,0:T(2,128)(2,1)S(1)}, u32[]{:S(2)}, u32[]{:S(2)}) async-start(bf16[128,2,5376]{2,1,0:T(2,128)(2,1)} %pack_rows.1), calls=%async_computation | async-start | bytes 5505024 | tf_op jit(solution)/shard_map/all_to_all | solution.py:526
  18.4 0.0 collective-permute-done.1.from_cross_ref
  18.4 0.0 copy-start
  18.5 0.0 collective-permute-done.from_same_ref
  18.5 1.1 %slice.8 = bf16[16,10240]{1,0:T(8,128)(2,1)S(1)} slice(bf16[16,13824]{1,0:T(8,128)(2,1)} %collective-permute-done.from_same_ref), slice={[0:16], [3584:13824]} | slice | bytes 655360 | tf_op jit(solution)/shard_map/slice | solution.py:530
  19.6 0.9 %pad_maximum_fusion = bf16[32,10240]{1,0:T(8,128)(2,1)} fusion(bf16[16,10240]{1,0:T(8,128)(2,1)S(1)} %slice.9, bf16[16,10240]{1,0:T(8,128)(2,1)S(1)} %slice.8), kind=kLoop, calls=%fused_computation | loop fusion | flops 1310720 | bytes 1310720 | tf_op jit(solution)/shard_map/concatenate | solution.py:530
  20.5 1.1 %collective-permute-start.2 = (bf16[32,10240]{1,0:T(8,128)(2,1)}, bf16[32,10240]{1,0:T(8,128)(2,1)}, u32[]{:S(2)}, u32[]{:S(2)}) collective-permute-start(bf16[32,10240]{1,0:T(8,128)(2,1)} %pad_maximum_fusion), channel_id=1, source_target_pairs={{0,1},{1,0},{2,3},{3,2},{4,5},{5,4},{6,7},{7,6},{8,9},{9,8},{10,11... | collective-permute-start | bytes 1966088 | tf_op jit(solution)/shard_map/ppermute | solution.py:531
  21.5 2.1 %collective-permute-done.2.other_ref = bf16[32,10240]{1,0:T(8,128)(2,1)} collective-permute-done((bf16[32,10240]{1,0:T(8,128)(2,1)}, bf16[32,10240]{1,0:T(8,128)(2,1)}, u32[]{:S(2)}, u32[]{:S(2)}) %collective-permute-start.2) | collective-permute-done | bytes 655392 | tf_op jit(solution)/shard_map/ppermute | solution.py:531
  23.6 0.0 copy-done.3
  23.6 1.0 %copy-done.1 = bf16[16,13824]{1,0:T(8,128)(2,1)S(1)} copy-done((bf16[16,13824]{1,0:T(8,128)(2,1)S(1)}, bf16[16,13824]{1,0:T(8,128)(2,1)}, u32[]{:S(2)}) %copy-start.1) | copy-done | bytes 442392
  24.6 7.7 %query_latent.1 = (bf16[32,16,512]{2,1,0:T(8,128)(2,1)S(1)}, bf16[16,16,512]{2,1,0:T(8,128)(2,1)}, bf16[16,16,512]{2,1,0:T(8,128)(2,1)}) custom-call(s32[1]{0:T(128)} %bitcast.rep_ref, bf16[16,8192]{1,0:T(8,128)(2,1)} %nope_ref.3, bf16[16,1536]{1,0:T(8,128)(2,1)S(1)} %copy-done.3, bf16[16,13824]{1,0:T(8,128)(2,1)} %collective-permute-done.from_same_ref, ...), custom_call_target="tpu_custom_call" | custom-call | flops 20000000000 | bytes 1024 | tf_op jit(solution)/shard_map/query_latent/pallas_call | solution.py:373
  32.3 0.6 picks.1
  32.9 0.8 collective-permute-start.3
  33.7 1.8 %collective-permute-start.4 = (bf16[16,16,512]{2,1,0:T(8,128)(2,1)}, bf16[16,16,512]{2,1,0:T(8,128)(2,1)}, u32[]{:S(2)}, u32[]{:S(2)}) collective-permute-start(bf16[16,16,512]{2,1,0:T(8,128)(2,1)} %get-tuple-element.38), channel_id=1, source_target_pairs={{0,66},{1,67},{2,64},{3,65},{4,70},{5,71},{6,68},{7,69},{8,74},{9,... | collective-permute-start | bytes 786440 | tf_op jit(solution)/shard_map/ppermute | solution.py:536
  35.5 20.4 %all-to-all-done.x_ref = bf16[128,2,5376]{2,1,0:T(2,128)(2,1)S(1)} async-done(((bf16[128,2,5376]{2,1,0:T(2,128)(2,1)}), bf16[128,2,5376]{2,1,0:T(2,128)(2,1)S(1)}, u32[]{:S(2)}, u32[]{:S(2)}) %all-to-all-start) | async-done | bytes 2752544 | tf_op jit(solution)/shard_map/all_to_all | solution.py:526
  55.9 9.2 %expert_rows.1 = bf16[128,2,1536]{2,1,0:T(2,128)(2,1)} custom-call(bf16[128,2,5376]{2,1,0:T(2,128)(2,1)S(1)} %all-to-all-done.x_ref, bf16[1,3584,2048]{2,1,0:T(8,128)(2,1)} %w_ref.1), custom_call_target="tpu_custom_call" | custom-call | flops 5637144576 | bytes 18874368 | tf_op jit(solution)/shard_map/expert_rows/pallas_call | solution.py:223
  65.1 0.0 collective-permute-done.3.same_ref
  65.1 0.0 collective-permute-done.4.cross_ref
  65.1 4.7 %all-to-all-start.1 = ((bf16[128,2,1536]{2,1,0:T(2,128)(2,1)}), bf16[128,2,1536]{2,1,0:T(2,128)(2,1)S(1)}, u32[]{:S(2)}, u32[]{:S(2)}) async-start(bf16[128,2,1536]{2,1,0:T(2,128)(2,1)} %expert_rows.1), calls=%async_computation.1 | async-start | bytes 1572864 | tf_op jit(solution)/shard_map/all_to_all | solution.py:545
  69.8 0.0 copy-done.6
  69.9 0.2 reshape.12.rope_ref
  70.1 0.1 copy.16.weight_ref
  70.2 12.9 %attend_rows.1 = bf16[16,32768]{1,0:T(8,128)(2,1)} custom-call(s32[16]{0:T(128)S(1)} %copy-done.5, s32[1]{0:T(128)} %bitcast.rep_ref, bf16[32,16,512]{2,1,0:T(8,128)(2,1)S(1)} %get-tuple-element.35.own_ref, bf16[16,16,512]{2,1,0:T(8,128)(2,1)} %collective-permute-done.3.same_ref, bf16[16,16,512]{2,1,0:T(8,128)(2,1)} %collective-permute-done.4.cross_ref, ...), custom_call_target="tpu_custom_call" | custom-call | flops 427819008 | bytes 6291456 | tf_op jit(solution)/shard_map/attend_rows/pallas_call | solution.py:472
  83.1 3.3 %all-to-all-done.1.back_ref = bf16[128,2,1536]{2,1,0:T(2,128)(2,1)S(1)} async-done(((bf16[128,2,1536]{2,1,0:T(2,128)(2,1)}), bf16[128,2,1536]{2,1,0:T(2,128)(2,1)S(1)}, u32[]{:S(2)}, u32[]{:S(2)}) %all-to-all-start.1) | async-done | bytes 786464 | tf_op jit(solution)/shard_map/all_to_all | solution.py:545
  86.4 1.3 %unpack_rows.1 = bf16[16,8192]{1,0:T(8,128)(2,1)} custom-call(bf16[128,256]{1,0:T(8,128)(2,1)S(1)} %get-tuple-element.41.pick_a_ref, bf16[128,128]{1,0:T(8,128)(2,1)S(1)} %get-tuple-element.42.pick_b_ref, f32[16,8]{1,0:T(8,128)S(1)} %copy.16.weight_ref, bf16[128,2,1536]{2,1,0:T(2,128)(2,1)S(1)} %all-to-all-done.1.back_ref), custom_call_target="tpu_custom_call" | custom-call | flops 100663296 | bytes 2097152 | tf_op jit(solution)/shard_map/unpack_rows/pallas_call | solution.py:286
  (10 shorter events, 0.0 us)
Async XLA Ops:
  0.6 5.7 %copy-start.2 = (bf16[16,3584]{1,0:T(8,128)(2,1)S(1)}, bf16[16,3584]{1,0:T(8,128)(2,1)}, u32[]{:S(2)}) copy-start(bf16[16,3584]{1,0:T(8,128)(2,1)} %x_ref) | copy-start | bytes 344068
  2.9 15.5 %collective-permute-start.1 = (bf16[16,13824]{1,0:T(8,128)(2,1)}, bf16[16,13824]{1,0:T(8,128)(2,1)S(1)}, u32[]{:S(2)}, u32[]{:S(2)}) collective-permute-start(bf16[16,13824]{1,0:T(8,128)(2,1)} %get-tuple-element.29), channel_id=1, source_target_pairs={{0,66},{1,67},{2,64},{3,65},{4,70},{5,71},{6,68},{7,69},{8,74},{9,... | collective-permute-start | bytes 1327112 | tf_op jit(solution)/shard_map/ppermute | solution.py:529
  6.3 12.1 %collective-permute-start = (bf16[16,13824]{1,0:T(8,128)(2,1)}, bf16[16,13824]{1,0:T(8,128)(2,1)}, u32[]{:S(2)}, u32[]{:S(2)}) collective-permute-start(bf16[16,13824]{1,0:T(8,128)(2,1)} %get-tuple-element.28), channel_id=1, source_target_pairs={{0,64},{1,65},{2,66},{3,67},{4,68},{5,69},{6,70},{7,71},{8,72},{9,... | collective-permute-start | bytes 1327112 | tf_op jit(solution)/shard_map/ppermute | solution.py:528
  8.4 15.2 %copy-start.3 = (bf16[16,1536]{1,0:T(8,128)(2,1)S(1)}, bf16[16,1536]{1,0:T(8,128)(2,1)}, u32[]{:S(2)}) copy-start(bf16[16,1536]{1,0:T(8,128)(2,1)} %comp_ref.3) | copy-start | bytes 147460
  8.4 47.5 %all-to-all-start = ((bf16[128,2,5376]{2,1,0:T(2,128)(2,1)}), bf16[128,2,5376]{2,1,0:T(2,128)(2,1)S(1)}, u32[]{:S(2)}, u32[]{:S(2)}) async-start(bf16[128,2,5376]{2,1,0:T(2,128)(2,1)} %pack_rows.1), calls=%async_computation | async-start | bytes 5505024 | tf_op jit(solution)/shard_map/all_to_all | solution.py:526
  18.4 5.2 %copy-start = (bf16[16,13824]{1,0:T(8,128)(2,1)}, bf16[16,13824]{1,0:T(8,128)(2,1)S(1)}, u32[]{:S(2)}) copy-start(bf16[16,13824]{1,0:T(8,128)(2,1)S(1)} %collective-permute-done.1.from_cross_ref) | copy-start | bytes 1327108
  20.5 3.1 %collective-permute-start.2 = (bf16[32,10240]{1,0:T(8,128)(2,1)}, bf16[32,10240]{1,0:T(8,128)(2,1)}, u32[]{:S(2)}, u32[]{:S(2)}) collective-permute-start(bf16[32,10240]{1,0:T(8,128)(2,1)} %pad_maximum_fusion), channel_id=1, source_target_pairs={{0,1},{1,0},{2,3},{3,2},{4,5},{5,4},{6,7},{7,6},{8,9},{9,8},{10,11... | collective-permute-start | bytes 1966088 | tf_op jit(solution)/shard_map/ppermute | solution.py:531
  23.6 1.0 %copy-start.1 = (bf16[16,13824]{1,0:T(8,128)(2,1)S(1)}, bf16[16,13824]{1,0:T(8,128)(2,1)}, u32[]{:S(2)}) copy-start(bf16[16,13824]{1,0:T(8,128)(2,1)} %copy-done) | copy-start | bytes 1327108
  24.6 7.7 %copy-start.4 = (s32[16,8]{0,1:T(8,128)S(1)}, s32[16,8]{0,1:T(8,128)}, u32[]{:S(2)}) copy-start(s32[16,8]{0,1:T(8,128)} %param.25) | copy-start | bytes 1540
  32.9 32.2 %collective-permute-start.3 = (bf16[16,16,512]{2,1,0:T(8,128)(2,1)}, bf16[16,16,512]{2,1,0:T(8,128)(2,1)}, u32[]{:S(2)}, u32[]{:S(2)}) collective-permute-start(bf16[16,16,512]{2,1,0:T(8,128)(2,1)} %get-tuple-element.37), channel_id=1, source_target_pairs={{0,64},{1,65},{2,66},{3,67},{4,68},{5,69},{6,70},{7,71},{8,72},{9,... | collective-permute-start | bytes 786440 | tf_op jit(solution)/shard_map/ppermute | solution.py:535
  33.7 31.4 %collective-permute-start.4 = (bf16[16,16,512]{2,1,0:T(8,128)(2,1)}, bf16[16,16,512]{2,1,0:T(8,128)(2,1)}, u32[]{:S(2)}, u32[]{:S(2)}) collective-permute-start(bf16[16,16,512]{2,1,0:T(8,128)(2,1)} %get-tuple-element.38), channel_id=1, source_target_pairs={{0,66},{1,67},{2,64},{3,65},{4,70},{5,71},{6,68},{7,69},{8,74},{9,... | collective-permute-start | bytes 786440 | tf_op jit(solution)/shard_map/ppermute | solution.py:536
  55.9 14.0 %copy-start.6 = (bf16[16,4096]{1,0:T(8,128)(2,1)S(1)}, bf16[16,4096]{1,0:T(8,128)(2,1)}, u32[]{:S(2)}) copy-start(bf16[16,4096]{1,0:T(8,128)(2,1)} %param.15) | copy-start | bytes 393220
  55.9 14.2 %copy-start.7 = (f32[16,8]{0,1:T(8,128)S(1)}, f32[16,8]{0,1:T(8,128)}, u32[]{:S(2)}) copy-start(f32[16,8]{0,1:T(8,128)} %param.26) | copy-start | bytes 1540
  55.9 14.3 %copy-start.5 = (s32[16]{0:T(128)S(1)}, s32[16]{0:T(128)}, u32[]{:S(2)}) copy-start(s32[16]{0:T(128)} %lengths_ref.1) | copy-start | bytes 196
  65.1 21.2 %all-to-all-start.1 = ((bf16[128,2,1536]{2,1,0:T(2,128)(2,1)}), bf16[128,2,1536]{2,1,0:T(2,128)(2,1)S(1)}, u32[]{:S(2)}, u32[]{:S(2)}) async-start(bf16[128,2,1536]{2,1,0:T(2,128)(2,1)} %expert_rows.1), calls=%async_computation.1 | async-start | bytes 1572864 | tf_op jit(solution)/shard_map/all_to_all | solution.py:545

commit v5 on v3

--- a/solution.py
+++ b/solution.py
@@ -483,8 +483,8 @@
             ],
             out_specs=pl.BlockSpec((ROWS, HEADS * LATENT), lambda s, *_: (0, 0)),
             scratch_shapes=[
-                pltpu.VMEM((LANES, HEADS * ROWS, 128), f32),
-                pltpu.VMEM((LANES, ROWS * HEADS, 128), f32),
+                pltpu.VMEM((LANES, (HEADS + 1) * ROWS, 128), f32),
+                pltpu.VMEM((LANES, (ROWS + 1) * HEADS, 128), f32),
             ],
         ),
         compiler_params=params(40),

time: 88.4 us -> 88.4 us (level)
  no operation moved by 1% of the time
where the time goes in v5:
time: 88.4 us; the launch traced here: 87.9 us
  Pallas kernels  36.3 us (41%)
  waiting for transfers between devices  25.8 us (29%)
  starting transfers between devices  21.7 us (25%)
  local copies, waits for them, and re-layouts  2.5 us (3%)
    all_to_all x1, waiting for transfers between devices, on_device(): arrived_rows = lax.all_to_all(leaving_rows, AXES, 0, 0, tiled=True)  20.4 us
    pallas_call x1, Pallas kernels, attend(): pl.pallas_call(attend_kernel, out_shape=jax.ShapeDtypeStruct((ROWS, HEADS...  12.9 us
    all_to_all x1, starting transfers between devices, on_device(): arrived_rows = lax.all_to_all(leaving_rows, AXES, 0, 0, tiled=True)  9.95 us
    pallas_call x1, Pallas kernels, expert(): pl.pallas_call(expert_kernel, out_shape=pltpu.HBM((EXPERTS, 2, TILES * ST...  9.46 us
    pallas_call x1, Pallas kernels, query_part(): pl.pallas_call(query_kernel, out_shape=(jax.ShapeDtypeStruct((HALF, ROWS,...  7.71 us
    all_to_all x1, starting transfers between devices, on_device(): back = lax.all_to_all(activation, AXES, 0, 0, tiled=True)  4.7 us
    ppermute x1, starting transfers between devices, on_device(): from_cross = lax.ppermute(cross, AXES, to_cross)  3.39 us
    all_to_all x1, waiting for transfers between devices, on_device(): back = lax.all_to_all(activation, AXES, 0, 0, tiled=True)  3.31 us
  transfers between devices with their start and end apart: 7, of which 3 were waited for; matrix products, arithmetic and copies ran while one was open for 3% of the time, Pallas kernels for 37%

profile of v5, /device:TPU:1, one launch (start us, length us, event | category | flops | bytes accessed | tf_op | source)
XLA Modules:
  0.0 87.9 jit_solution(9609608741949200133)
XLA Ops:
  0.6 0.0 copy-start.2
  0.6 2.3 %payloads.1 = (bf16[16,13824]{1,0:T(8,128)(2,1)}, bf16[16,13824]{1,0:T(8,128)(2,1)}, bf16[256,16]{1,0:T(8,128)(2,1)S(1)}, bf16[128,16]{1,0:T(8,128)(2,1)S(1)}) custom-call(s32[8,16]{1,0:T(8,128)} %bitcast.8, bf16[16,8192]{1,0:T(8,128)(2,1)} %nope_ref.3, bf16[16,1536]{1,0:T(8,128)(2,1)} %comp_ref.3, bf16[64,8192]{1,0:T(8,128)(2,1)} %bitcast.10, ...), custom_call_target="tpu_custom_call" | custom-call | flops 1024 | bytes 1048576 | tf_op jit(solution)/shard_map/payloads/pallas_call | solution.py:124
  2.9 3.4 %collective-permute-start.1 = (bf16[16,13824]{1,0:T(8,128)(2,1)}, bf16[16,13824]{1,0:T(8,128)(2,1)S(1)}, u32[]{:S(2)}, u32[]{:S(2)}) collective-permute-start(bf16[16,13824]{1,0:T(8,128)(2,1)} %get-tuple-element.29), channel_id=1, source_target_pairs={{0,66},{1,67},{2,64},{3,65},{4,70},{5,71},{6,68},{7,69},{8,74},{9,... | collective-permute-start | bytes 1327112 | tf_op jit(solution)/shard_map/ppermute | solution.py:528
  6.3 0.0 collective-permute-start
  6.3 0.0 copy-done.2
  6.3 2.1 %pack_rows.1 = bf16[128,2,5376]{2,1,0:T(2,128)(2,1)} custom-call(bf16[256,16]{1,0:T(8,128)(2,1)S(1)} %get-tuple-element.23.a_ref, bf16[128,16]{1,0:T(8,128)(2,1)S(1)} %get-tuple-element.24.b_ref, bf16[16,3584]{1,0:T(8,128)(2,1)S(1)} %copy-done.2), custom_call_target="tpu_custom_call" | custom-call | flops 44040192 | bytes 3145728 | tf_op jit(solution)/shard_map/pack_rows/pallas_call | solution.py:163
  8.4 0.0 copy-start.3
  8.4 10.0 %all-to-all-start = ((bf16[128,2,5376]{2,1,0:T(2,128)(2,1)}), bf16[128,2,5376]{2,1,0:T(2,128)(2,1)S(1)}, u32[]{:S(2)}, u32[]{:S(2)}) async-start(bf16[128,2,5376]{2,1,0:T(2,128)(2,1)} %pack_rows.1), calls=%async_computation | async-start | bytes 5505024 | tf_op jit(solution)/shard_map/all_to_all | solution.py:525
  18.4 0.0 collective-permute-done.1.from_cross_ref
  18.4 0.0 copy-start
  18.5 0.0 collective-permute-done.from_same_ref
  18.5 1.1 %slice.8 = bf16[16,10240]{1,0:T(8,128)(2,1)S(1)} slice(bf16[16,13824]{1,0:T(8,128)(2,1)} %collective-permute-done.from_same_ref), slice={[0:16], [3584:13824]} | slice | bytes 655360 | tf_op jit(solution)/shard_map/slice | solution.py:529
  19.6 0.9 %pad_maximum_fusion = bf16[32,10240]{1,0:T(8,128)(2,1)} fusion(bf16[16,10240]{1,0:T(8,128)(2,1)S(1)} %slice.9, bf16[16,10240]{1,0:T(8,128)(2,1)S(1)} %slice.8), kind=kLoop, calls=%fused_computation | loop fusion | flops 1310720 | bytes 1310720 | tf_op jit(solution)/shard_map/concatenate | solution.py:529
  20.5 1.1 %collective-permute-start.2 = (bf16[32,10240]{1,0:T(8,128)(2,1)}, bf16[32,10240]{1,0:T(8,128)(2,1)}, u32[]{:S(2)}, u32[]{:S(2)}) collective-permute-start(bf16[32,10240]{1,0:T(8,128)(2,1)} %pad_maximum_fusion), channel_id=1, source_target_pairs={{0,1},{1,0},{2,3},{3,2},{4,5},{5,4},{6,7},{7,6},{8,9},{9,8},{10,11... | collective-permute-start | bytes 1966088 | tf_op jit(solution)/shard_map/ppermute | solution.py:530
  21.5 2.1 %collective-permute-done.2.other_ref = bf16[32,10240]{1,0:T(8,128)(2,1)} collective-permute-done((bf16[32,10240]{1,0:T(8,128)(2,1)}, bf16[32,10240]{1,0:T(8,128)(2,1)}, u32[]{:S(2)}, u32[]{:S(2)}) %collective-permute-start.2) | collective-permute-done | bytes 655392 | tf_op jit(solution)/shard_map/ppermute | solution.py:530
  23.6 0.0 copy-done
  23.6 1.0 %copy-done.1 = bf16[16,13824]{1,0:T(8,128)(2,1)S(1)} copy-done((bf16[16,13824]{1,0:T(8,128)(2,1)S(1)}, bf16[16,13824]{1,0:T(8,128)(2,1)}, u32[]{:S(2)}) %copy-start.1) | copy-done | bytes 442392
  24.6 7.7 %query_latent.1 = (bf16[32,16,512]{2,1,0:T(8,128)(2,1)S(1)}, bf16[16,16,512]{2,1,0:T(8,128)(2,1)}, bf16[16,16,512]{2,1,0:T(8,128)(2,1)}) custom-call(s32[1]{0:T(128)} %bitcast.rep_ref, bf16[16,8192]{1,0:T(8,128)(2,1)} %nope_ref.3, bf16[16,1536]{1,0:T(8,128)(2,1)S(1)} %copy-done.3, bf16[16,13824]{1,0:T(8,128)(2,1)} %collective-permute-done.from_same_ref, ...), custom_call_target="tpu_custom_call" | custom-call | flops 20000000000 | bytes 1024 | tf_op jit(solution)/shard_map/query_latent/pallas_call | solution.py:372
  32.3 0.6 picks.1
  32.9 0.8 collective-permute-start.3
  33.7 1.8 %collective-permute-start.4 = (bf16[16,16,512]{2,1,0:T(8,128)(2,1)}, bf16[16,16,512]{2,1,0:T(8,128)(2,1)}, u32[]{:S(2)}, u32[]{:S(2)}) collective-permute-start(bf16[16,16,512]{2,1,0:T(8,128)(2,1)} %get-tuple-element.38), channel_id=1, source_target_pairs={{0,66},{1,67},{2,64},{3,65},{4,70},{5,71},{6,68},{7,69},{8,74},{9,... | collective-permute-start | bytes 786440 | tf_op jit(solution)/shard_map/ppermute | solution.py:535
  35.5 20.4 %all-to-all-done.x_ref = bf16[128,2,5376]{2,1,0:T(2,128)(2,1)S(1)} async-done(((bf16[128,2,5376]{2,1,0:T(2,128)(2,1)}), bf16[128,2,5376]{2,1,0:T(2,128)(2,1)S(1)}, u32[]{:S(2)}, u32[]{:S(2)}) %all-to-all-start) | async-done | bytes 2752544 | tf_op jit(solution)/shard_map/all_to_all | solution.py:525
  55.9 9.5 %expert_rows.1 = bf16[128,2,1536]{2,1,0:T(2,128)(2,1)} custom-call(bf16[128,2,5376]{2,1,0:T(2,128)(2,1)S(1)} %all-to-all-done.x_ref, bf16[1,3584,2048]{2,1,0:T(8,128)(2,1)} %w_ref.1), custom_call_target="tpu_custom_call" | custom-call | flops 5637144576 | bytes 18874368 | tf_op jit(solution)/shard_map/expert_rows/pallas_call | solution.py:222
  65.4 0.0 collective-permute-done.3.same_ref
  65.4 0.0 collective-permute-done.4.cross_ref
  65.4 4.7 %all-to-all-start.1 = ((bf16[128,2,1536]{2,1,0:T(2,128)(2,1)}), bf16[128,2,1536]{2,1,0:T(2,128)(2,1)S(1)}, u32[]{:S(2)}, u32[]{:S(2)}) async-start(bf16[128,2,1536]{2,1,0:T(2,128)(2,1)} %expert_rows.1), calls=%async_computation.1 | async-start | bytes 1572864 | tf_op jit(solution)/shard_map/all_to_all | solution.py:544
  70.1 0.2 reshape.12.rope_ref
  70.4 0.1 copy.16.weight_ref
  70.4 0.0 copy-done.5
  70.4 12.9 %attend_rows.1 = bf16[16,32768]{1,0:T(8,128)(2,1)} custom-call(s32[16]{0:T(128)S(1)} %copy-done.5, s32[1]{0:T(128)} %bitcast.rep_ref, bf16[32,16,512]{2,1,0:T(8,128)(2,1)S(1)} %get-tuple-element.35.own_ref, bf16[16,16,512]{2,1,0:T(8,128)(2,1)} %collective-permute-done.3.same_ref, bf16[16,16,512]{2,1,0:T(8,128)(2,1)} %collective-permute-done.4.cross_ref, ...), custom_call_target="tpu_custom_call" | custom-call | flops 427819008 | bytes 6291456 | tf_op jit(solution)/shard_map/attend_rows/pallas_call | solution.py:471
  83.3 3.3 %all-to-all-done.1.back_ref = bf16[128,2,1536]{2,1,0:T(2,128)(2,1)S(1)} async-done(((bf16[128,2,1536]{2,1,0:T(2,128)(2,1)}), bf16[128,2,1536]{2,1,0:T(2,128)(2,1)S(1)}, u32[]{:S(2)}, u32[]{:S(2)}) %all-to-all-start.1) | async-done | bytes 786464 | tf_op jit(solution)/shard_map/all_to_all | solution.py:544
  86.6 1.3 %unpack_rows.1 = bf16[16,8192]{1,0:T(8,128)(2,1)} custom-call(bf16[128,256]{1,0:T(8,128)(2,1)S(1)} %get-tuple-element.41.pick_a_ref, bf16[128,128]{1,0:T(8,128)(2,1)S(1)} %get-tuple-element.42.pick_b_ref, f32[16,8]{1,0:T(8,128)S(1)} %copy.16.weight_ref, bf16[128,2,1536]{2,1,0:T(2,128)(2,1)S(1)} %all-to-all-done.1.back_ref), custom_call_target="tpu_custom_call" | custom-call | flops 100663296 | bytes 2097152 | tf_op jit(solution)/shard_map/unpack_rows/pallas_call | solution.py:285
  (10 shorter events, 0.0 us)
Async XLA Ops:
  0.6 5.7 %copy-start.2 = (bf16[16,3584]{1,0:T(8,128)(2,1)S(1)}, bf16[16,3584]{1,0:T(8,128)(2,1)}, u32[]{:S(2)}) copy-start(bf16[16,3584]{1,0:T(8,128)(2,1)} %x_ref) | copy-start | bytes 344068
  2.9 15.5 %collective-permute-start.1 = (bf16[16,13824]{1,0:T(8,128)(2,1)}, bf16[16,13824]{1,0:T(8,128)(2,1)S(1)}, u32[]{:S(2)}, u32[]{:S(2)}) collective-permute-start(bf16[16,13824]{1,0:T(8,128)(2,1)} %get-tuple-element.29), channel_id=1, source_target_pairs={{0,66},{1,67},{2,64},{3,65},{4,70},{5,71},{6,68},{7,69},{8,74},{9,... | collective-permute-start | bytes 1327112 | tf_op jit(solution)/shard_map/ppermute | solution.py:528
  6.3 12.1 %collective-permute-start = (bf16[16,13824]{1,0:T(8,128)(2,1)}, bf16[16,13824]{1,0:T(8,128)(2,1)}, u32[]{:S(2)}, u32[]{:S(2)}) collective-permute-start(bf16[16,13824]{1,0:T(8,128)(2,1)} %get-tuple-element.28), channel_id=1, source_target_pairs={{0,64},{1,65},{2,66},{3,67},{4,68},{5,69},{6,70},{7,71},{8,72},{9,... | collective-permute-start | bytes 1327112 | tf_op jit(solution)/shard_map/ppermute | solution.py:527
  8.4 15.2 %copy-start.3 = (bf16[16,1536]{1,0:T(8,128)(2,1)S(1)}, bf16[16,1536]{1,0:T(8,128)(2,1)}, u32[]{:S(2)}) copy-start(bf16[16,1536]{1,0:T(8,128)(2,1)} %comp_ref.3) | copy-start | bytes 147460
  8.4 47.5 %all-to-all-start = ((bf16[128,2,5376]{2,1,0:T(2,128)(2,1)}), bf16[128,2,5376]{2,1,0:T(2,128)(2,1)S(1)}, u32[]{:S(2)}, u32[]{:S(2)}) async-start(bf16[128,2,5376]{2,1,0:T(2,128)(2,1)} %pack_rows.1), calls=%async_computation | async-start | bytes 5505024 | tf_op jit(solution)/shard_map/all_to_all | solution.py:525
  18.4 5.2 %copy-start = (bf16[16,13824]{1,0:T(8,128)(2,1)}, bf16[16,13824]{1,0:T(8,128)(2,1)S(1)}, u32[]{:S(2)}) copy-start(bf16[16,13824]{1,0:T(8,128)(2,1)S(1)} %collective-permute-done.1.from_cross_ref) | copy-start | bytes 1327108
  20.5 3.1 %collective-permute-start.2 = (bf16[32,10240]{1,0:T(8,128)(2,1)}, bf16[32,10240]{1,0:T(8,128)(2,1)}, u32[]{:S(2)}, u32[]{:S(2)}) collective-permute-start(bf16[32,10240]{1,0:T(8,128)(2,1)} %pad_maximum_fusion), channel_id=1, source_target_pairs={{0,1},{1,0},{2,3},{3,2},{4,5},{5,4},{6,7},{7,6},{8,9},{9,8},{10,11... | collective-permute-start | bytes 1966088 | tf_op jit(solution)/shard_map/ppermute | solution.py:530
  23.6 1.0 %copy-start.1 = (bf16[16,13824]{1,0:T(8,128)(2,1)S(1)}, bf16[16,13824]{1,0:T(8,128)(2,1)}, u32[]{:S(2)}) copy-start(bf16[16,13824]{1,0:T(8,128)(2,1)} %copy-done) | copy-start | bytes 1327108
  24.6 7.7 %copy-start.4 = (s32[16,8]{0,1:T(8,128)S(1)}, s32[16,8]{0,1:T(8,128)}, u32[]{:S(2)}) copy-start(s32[16,8]{0,1:T(8,128)} %param.25) | copy-start | bytes 1540
  32.9 32.4 %collective-permute-start.3 = (bf16[16,16,512]{2,1,0:T(8,128)(2,1)}, bf16[16,16,512]{2,1,0:T(8,128)(2,1)}, u32[]{:S(2)}, u32[]{:S(2)}) collective-permute-start(bf16[16,16,512]{2,1,0:T(8,128)(2,1)} %get-tuple-element.37), channel_id=1, source_target_pairs={{0,64},{1,65},{2,66},{3,67},{4,68},{5,69},{6,70},{7,71},{8,72},{9,... | collective-permute-start | bytes 786440 | tf_op jit(solution)/shard_map/ppermute | solution.py:534
  33.7 31.7 %collective-permute-start.4 = (bf16[16,16,512]{2,1,0:T(8,128)(2,1)}, bf16[16,16,512]{2,1,0:T(8,128)(2,1)}, u32[]{:S(2)}, u32[]{:S(2)}) collective-permute-start(bf16[16,16,512]{2,1,0:T(8,128)(2,1)} %get-tuple-element.38), channel_id=1, source_target_pairs={{0,66},{1,67},{2,64},{3,65},{4,70},{5,71},{6,68},{7,69},{8,74},{9,... | collective-permute-start | bytes 786440 | tf_op jit(solution)/shard_map/ppermute | solution.py:535
  55.9 14.2 %copy-start.6 = (bf16[16,4096]{1,0:T(8,128)(2,1)S(1)}, bf16[16,4096]{1,0:T(8,128)(2,1)}, u32[]{:S(2)}) copy-start(bf16[16,4096]{1,0:T(8,128)(2,1)} %param.15) | copy-start | bytes 393220
  55.9 14.5 %copy-start.7 = (f32[16,8]{0,1:T(8,128)S(1)}, f32[16,8]{0,1:T(8,128)}, u32[]{:S(2)}) copy-start(f32[16,8]{0,1:T(8,128)} %param.26) | copy-start | bytes 1540
  55.9 14.5 %copy-start.5 = (s32[16]{0:T(128)S(1)}, s32[16]{0:T(128)}, u32[]{:S(2)}) copy-start(s32[16]{0:T(128)} %lengths_ref.1) | copy-start | bytes 196
  65.4 21.2 %all-to-all-start.1 = ((bf16[128,2,1536]{2,1,0:T(2,128)(2,1)}), bf16[128,2,1536]{2,1,0:T(2,128)(2,1)S(1)}, u32[]{:S(2)}, u32[]{:S(2)}) async-start(bf16[128,2,1536]{2,1,0:T(2,128)(2,1)} %expert_rows.1), calls=%async_computation.1 | async-start | bytes 1572864 | tf_op jit(solution)/shard_map/all_to_all | solution.py:544
